TPU v7x, 256 devices: a whole 4x4x8 slice. The times are simulated.
256 devices in a mesh: section: 8 (over x, core), dp: 16 (over y_hi, z), mp: 2 (over y_lo).
Axes of the slice: x: 4, y: 4 (y_hi: 2, y_lo: 2; y = y_hi * 2 + y_lo), z: 8, core: 2. Of those that a mesh axis runs over, the one named last changes fastest.
Arguments:
- nbr_states: bfloat16 [4096, 8192], P('dp'), may hold values from -6 to 6
- kv_weight: bfloat16 [8192, 2, 4096], P(None, None, ('section', 'mp')), may hold values from -0.0625 to 0.0625
- queries: bfloat16 [4096, 4096], P('dp', ('section', 'mp')), may hold values from -36 to 36
- out_grad: bfloat16 [4096, 4096], P('dp', ('section', 'mp')), may hold values from -6 to 6
- citations: int32 [64, 2], P('dp'), may hold values from 0 to 31, as said below
Outputs:
- attended: bfloat16 [4096, 4096], P('dp', ('section', 'mp'))
- nbr_grad: bfloat16 [4096, 8192], P('dp', ('section', 'mp'))
Inputs may be any that keep to these rules, and one draw needn't show every extreme that they name: `citations`: owner of id i is i // 2. The two ids of one decoder block have different owners; all ids that the 4 blocks of one dp index cite from one owner are equal.
All inputs are finite; a program needn't handle non-finite values.
Results may differ from a plain program's by a relative error of at most 0.012.
The roundings to bfloat16 on the way count: a program that leaves them out, or rounds other values in their place, can miss the bound.
Values may be sent and summed in bfloat16 or wider, within the bound.
A program may use at most 128 MiB of HBM per device.

v0:
```python
import jax
import jax.numpy as jnp
from jax import lax
from jax.sharding import PartitionSpec as P

HS = 128
CH = 64
CL = 128
NCH_DEV = 2


def on_device(nbr_states, kv_weight, queries, out_grad, citations):
    owners = lax.axis_size("dp")
    model_width = kv_weight.shape[0]
    cols_here = kv_weight.shape[2]
    heads_here = cols_here // HS
    blocks_here = citations.shape[0]
    scaling = 1.0 / HS**0.5
    flat_weight = kv_weight.reshape(model_width, 2 * cols_here)
    own_rows = jnp.dot(nbr_states, flat_weight, preferred_element_type=jnp.float32).astype(
        jnp.bfloat16
    )
    own_rows = own_rows.reshape(NCH_DEV, CL, 2, cols_here)
    all_rows = lax.all_gather(own_rows, "dp", axis=0, tiled=True)
    neighbours = all_rows[citations]
    key_rows = neighbours[:, :, :, 0].reshape(blocks_here, 2 * CL, heads_here, HS)
    value_rows = neighbours[:, :, :, 1].reshape(blocks_here, 2 * CL, heads_here, HS)
    query_rows = queries.reshape(blocks_here, CH, heads_here, HS)
    out_rows = out_grad.reshape(blocks_here, CH, heads_here, HS)
    scores = (
        jnp.einsum("cqhd,ckhd->chqk", query_rows, key_rows, preferred_element_type=jnp.float32)
        * scaling
    )
    attn_prob = jax.nn.softmax(scores, axis=-1)
    rounded = attn_prob.astype(jnp.bfloat16)
    attended = jnp.einsum(
        "chqk,ckhd->cqhd", rounded, value_rows, preferred_element_type=jnp.float32
    )
    attended = attended.astype(jnp.bfloat16).reshape(blocks_here * CH, cols_here)
    value_grad = jnp.einsum(
        "chqk,cqhd->ckhd", rounded, out_rows, preferred_element_type=jnp.float32
    )
    prob_grad = jnp.einsum(
        "cqhd,ckhd->chqk", out_rows, value_rows, preferred_element_type=jnp.float32
    )
    score_grad = attn_prob * (prob_grad - jnp.sum(prob_grad * attn_prob, axis=-1, keepdims=True))
    score_grad = score_grad.astype(jnp.bfloat16)
    key_grad = (
        jnp.einsum("chqk,cqhd->ckhd", score_grad, query_rows, preferred_element_type=jnp.float32)
        * scaling
    )
    row_grads = jnp.stack(
        [
            key_grad.reshape(blocks_here, 2, CL, cols_here),
            value_grad.reshape(blocks_here, 2, CL, cols_here),
        ],
        axis=3,
    )
    all_blocks = NCH_DEV * owners
    block_onehot = (citations[:, :, None] == jnp.arange(all_blocks, dtype=jnp.int32)).astype(
        jnp.float32
    )
    every_grad = jnp.einsum(
        "cjn,cjtkx->ntkx", block_onehot, row_grads, precision=lax.Precision.HIGHEST
    )
    own_grad = lax.psum_scatter(every_grad, "dp", scatter_dimension=0, tiled=True)
    flat_grad = own_grad.astype(jnp.bfloat16).reshape(NCH_DEV * CL, 2 * cols_here)
    partial_value = lax.dot_general(
        flat_grad, flat_weight, (((1,), (1,)), ((), ())), preferred_element_type=jnp.float32
    )
    nbr_grad = lax.psum_scatter(
        partial_value, ("section", "mp"), scatter_dimension=1, tiled=True
    ).astype(jnp.bfloat16)
    return (attended, nbr_grad)


def solution(mesh):
    return jax.shard_map(
        on_device,
        mesh=mesh,
        in_specs=(
            P("dp", None),
            P(None, None, ("section", "mp")),
            P("dp", ("section", "mp")),
            P("dp", ("section", "mp")),
            P("dp", None),
        ),
        out_specs=(P("dp", ("section", "mp")), P("dp", ("section", "mp"))),
        check_vma=False,
    )
```

profile of v0, /device:TPU:1, one launch (start us, length us, event | category | flops | bytes accessed | tf_op | source)
XLA Modules:
  0.0 573.5 jit_solution(15565581052974075006)
XLA Ops:
  7.2 8.0 %copy.49 = bf16[1024,8,2,256]{3,1,2,0:T(8,128)(2,1)} copy(bf16[1024,8,2,256]{3,2,1,0:T(2,128)(2,1)} %bitcast.51) | data formatting | bytes 16777216
  15.2 7.0 %convolution_convert_fusion = bf16[256,512]{1,0:T(8,128)(2,1)S(1)} fusion(bf16[256,8192]{1,0:T(8,128)(2,1)} %param.5, bf16[8192,512]{1,0:T(8,128)(2,1)} %bitcast.49), kind=kOutput, calls=%fused_computation.14 | convolution fusion | flops 2147614720 | bytes 12845056 | tf_op jit(solution)/shard_map/dot_general | solution.py:20
  22.3 0.7 copy.27
  23.1 0.1 copy.28
  23.4 100.4 %all-gather.2.cloned.1.call-done = bf16[32,128,2,256]{3,1,2,0:T(8,128)(2,1)} async-done(((bf16[2,128,2,256]{3,1,2,0:T(8,128)(2,1)}), bf16[32,128,2,256]{3,1,2,0:T(8,128)(2,1)}) %all-gather.2.cloned.1.call-update) | async-done | bytes 4194320 | tf_op jit(solution)/shard_map/all_gather | solution.py:24
  123.8 2.8 gather_fusion
  126.6 0.1 slice_bitcast_fusion.1
  126.7 0.1 reshape_squeeze.7
  126.8 0.1 reshape_squeeze.6
  127.0 0.3 fusion.7
  127.3 1.5 fusion.23
  128.8 1.3 convolution_bitcast_fusion.1
  130.1 1.2 multiply_reduce_fusion
  131.3 2.4 fusion.4
  133.7 0.8 copy.38
  134.5 0.8 stack_reshape.6
  135.4 0.7 copy.41
  136.0 0.8 copy.40
  136.9 0.8 stack_reshape.7
  137.7 0.7 copy.42
  138.4 4.3 convolution_bitcast_fusion
  142.8 8.3 %copy.43 = f32[32,128,2,256]{3,1,2,0:T(8,128)} copy(f32[32,128,2,256]{3,0,2,1:T(8,128)S(1)} %convolution_bitcast_fusion) | data formatting | bytes 16777216 | tf_op jit(solution)/shard_map/cjn,cjtkx->ntkx/dot_general | solution.py:63
  151.1 218.9 %reduce-scatter.3.cloned.1.call-done = f32[2,128,2,256]{3,1,2,0:T(8,128)} async-done(((f32[32,128,2,256]{3,1,2,0:T(8,128)}), f32[2,128,2,256]{3,1,2,0:T(8,128)}) %reduce-scatter.3.cloned.1.call-update) | async-done | bytes 524304 | tf_op jit(solution)/shard_map/reduce_scatter | solution.py:66
  370.0 1.1 convert_element_type.27
  371.1 0.3 copy.44
  371.4 9.1 %fusion.24 = f32[256,8192]{1,0:T(8,128)} fusion(bf16[256,512]{1,0:T(8,128)(2,1)S(1)} %bitcast.53, bf16[8192,512]{1,0:T(8,128)(2,1)} %bitcast.50), kind=kOutput, calls=%fused_computation.40 | convolution fusion | flops 2147483648 | bytes 17039360 | tf_op jit(solution)/shard_map/dot_general | solution.py:68
  380.5 1.0 copy-done.2
  381.5 2.2 fusion.8
  383.7 0.1 copy.34
  383.8 0.7 copy.71
  384.5 180.7 %reduce-scatter.5.cloned.1.call-done = f32[256,512]{1,0:T(8,128)} async-done(((f32[256,8192]{1,0:T(8,128)}), f32[256,512]{1,0:T(8,128)}) %reduce-scatter.5.cloned.1.call-update) | async-done | bytes 524304 | tf_op jit(solution)/shard_map/reduce_scatter | solution.py:71
  565.2 1.8 convert_element_type.28
  (24 shorter events, 0.5 us)
Async XLA Ops:
  7.2 116.6 %all-gather.2.cloned.1.call-start = ((), (), s32[]{:S(2)}) async-start(), calls=%async_computation.2 | async-start | bytes 4456448 | tf_op jit(solution)/shard_map/all_gather | solution.py:24
  15.2 7.9 %copy-start.5 = (s32[4,2]{0,1:T(2,128)S(1)}, s32[4,2]{0,1:T(2,128)}, u32[]{:S(2)}) copy-start(s32[4,2]{0,1:T(2,128)} %param.9) | copy-start | bytes 100
  15.2 8.1 %copy-start.3 = (bf16[256,256]{1,0:T(8,128)(2,1)S(1)}, bf16[256,256]{1,0:T(8,128)(2,1)}, u32[]{:S(2)}) copy-start(bf16[256,256]{1,0:T(8,128)(2,1)} %param.7) | copy-start | bytes 393220
  15.2 8.1 %copy-start.4 = (bf16[256,256]{1,0:T(8,128)(2,1)S(1)}, bf16[256,256]{1,0:T(8,128)(2,1)}, u32[]{:S(2)}) copy-start(bf16[256,256]{1,0:T(8,128)(2,1)} %param.8) | copy-start | bytes 393220
  23.1 346.9 %reduce-scatter.3.cloned.1.call-start = ((), (), s32[]{:S(2)}) async-start(), calls=%async_computation.3 | async-start | bytes 8912896 | tf_op jit(solution)/shard_map/reduce_scatter | solution.py:66
  127.0 4.3 copy-start.1
  127.3 4.0 copy-start
  151.1 414.1 %reduce-scatter.5.cloned.1.call-start = ((), (), s32[]{:S(2)}) async-start(), calls=%async_computation.4 | async-start | bytes 8912896 | tf_op jit(solution)/shard_map/reduce_scatter | solution.py:71
  380.5 1.0 copy-start.2
Sparse Core Ops, SparseCore 0:
  23.2 100.5 all-gather.1
  151.2 218.7 reduce-scatter.2
  380.6 184.5 reduce-scatter.4
where the time goes:
time: 574 us; the launch traced here: 573 us
  waiting for transfers between devices  500 us (87%)
  matrix products  27.7 us (5%)
  local copies, waits for them, and re-layouts  27.3 us (5%)
  between operations  14 us (2%)
    reduce_scatter x1, waiting for transfers between devices, on_device(): lax.psum_scatter(every_grad, 'dp', scatter_dimension=0, tiled=True)  219 us
    reduce_scatter x1, waiting for transfers between devices, on_device(): lax.psum_scatter(partial_value, ('section', 'mp'), scatter_dimension=1, t...  181 us
    all_gather x1, waiting for transfers between devices, on_device(): all_rows = lax.all_gather(own_rows, 'dp', axis=0, tiled=True)  100 us
  transfers between devices with their start and end apart: 3, of which 3 were waited for; matrix products, arithmetic and copies ran while one was open for 1% of the time, Pallas kernels for 0%

commit v1 on v0

v1 whole, which is shorter than its diff:
```python
import functools

import jax
import jax.numpy as jnp
from jax import lax
from jax.experimental import pallas as pl
from jax.experimental.pallas import tpu as pltpu
from jax.sharding import PartitionSpec as P

HS = 128
CH = 64
CL = 128
NZ = 8
NX = 4
KC = 8
NEG = -1e30
BF = jnp.bfloat16
F32 = jnp.float32
NT = (((1,), (1,)), ((), ()))
NN = (((1,), (0,)), ((), ()))
TN = (((0,), (0,)), ((), ()))


def dot(a, b, dims):
    return lax.dot_general(a, b, dims, preferred_element_type=F32)


def kernel(
    cit_ref, q_ref, g_ref, x_hbm, w_hbm, att_ref, nbr_ref,
    X, W, acc, G, KV, info_out, info_in, E, DP, st_out, st_in, res_out, res_in,
    at_out, at_in, GR, yg_out, yg_in, kvg, cs_out, cs_in, R, by_in, RB,
    ax_in, ax_tmp, bx_in, bx_tmp, ay_out, ay_in,
    ld_sem, ag_send, ag_recv, kv_send, kv_recv, inf_send, inf_recv, st_send, st_recv,
    rs_send, rs_recv, at_send, at_recv, yg_send, yg_recv, cs_send, cs_recv,
    by_send, by_recv, ax_send, ax_recv, bx_send, bx_recv, ay_send, ay_recv,
):
    s, d, m = lax.axis_index("section"), lax.axis_index("dp"), lax.axis_index("mp")
    x, c = s // 2, s % 2
    yh, z = d // NZ, d % NZ
    depth = x_hbm.shape[1] // KC
    scaling = 1.0 / HS**0.5

    def at_z(zt):
        return {"dp": yh * NZ + zt}

    y_mate = {"dp": (1 - yh) * NZ + z}
    core_mate = {"section": x * 2 + (1 - c)}
    x_right = {"section": lax.rem(x + 1, NX) * 2 + c}
    x_left = {"section": lax.rem(x + NX - 1, NX) * 2 + c}
    m_mate = {"mp": 1 - m}

    def remote(src, dst, ssem, rsem, dev):
        return pltpu.make_async_remote_copy(
            src_ref=src, dst_ref=dst, send_sem=ssem, recv_sem=rsem,
            device_id=dev, device_id_type=pl.DeviceIdType.MESH,
        )

    def x_load(k):
        return pltpu.make_async_copy(
            x_hbm.at[:, pl.ds(pl.multiple_of(k * depth, depth), depth)], X.at[k], ld_sem.at[2, k]
        )

    def w_load(h, k):
        rows = pl.ds(pl.multiple_of(k * depth, depth), depth)
        return pltpu.make_async_copy(
            w_hbm.at[rows, pl.ds(h * 256, 256)], W.at[rows, pl.ds(h * 256, 256)], ld_sem.at[h, k]
        )

    def start_loads(k, _):
        x_load(k).start()
        w_load(0, k).start()
        return 0

    lax.fori_loop(0, KC, start_loads, 0)

    def start_loads_1(k, _):
        w_load(1, k).start()
        return 0

    lax.fori_loop(0, KC, start_loads_1, 0)

    barrier = pltpu.get_barrier_semaphore()
    for dev in [at_z(lax.rem(z + r, NZ)) for r in range(1, NZ)] + [
        y_mate, core_mate, x_right, x_left, m_mate
    ]:
        pl.semaphore_signal(barrier, inc=1, device_id=dev, device_id_type=pl.DeviceIdType.MESH)

    G[z, 0] = q_ref[...]
    G[z, 1] = g_ref[...]
    lane = lax.broadcasted_iota(jnp.int32, (16, 256), 1) // CH
    owner = lax.broadcasted_iota(jnp.int32, (16, 256), 0)
    ids = []
    for k in range(2):
        v = jnp.zeros((16, 256), jnp.int32)
        for b in range(4):
            v = jnp.where(lane == b, cit_ref[b, k], v)
        ids.append(v)
    second = (ids[0] == owner * 2 + 1) | (ids[1] == owner * 2 + 1)
    first = (ids[0] == owner * 2) | (ids[1] == owner * 2)
    cited = jnp.where(first | second, 1.0, 0.0).astype(F32)
    sel = jnp.where(second, 1.0, 0.0).astype(F32)
    sel = jnp.max(sel, axis=1, keepdims=True) + jnp.zeros((16, 256), F32)
    for t in range(NZ):
        for w in range(2):
            o = w * NZ + t
            info_out[t, w : w + 1, :] = cited[o : o + 1]
            info_out[t, 2 + w : 3 + w, :] = sel[o : o + 1]
        info_out[t, 4:8, :] = jnp.zeros((4, 256), F32)
    info_in[z] = info_out[z]
    pl.semaphore_wait(barrier, 12)

    def ag(direction, arr, t):
        if direction == 0:
            home, to = lax.rem(z - t + NZ, NZ), lax.rem(z + 1, NZ)
        else:
            home, to = lax.rem(z + t, NZ), lax.rem(z + NZ - 1, NZ)
        return remote(
            G.at[home, arr], G.at[home, arr],
            ag_send.at[direction, arr, t], ag_recv.at[direction, arr, t], at_z(to),
        )

    for direction in range(2):
        for arr in range(2):
            ag(direction, arr, 0).start()

    def info_copy(r):
        to = lax.rem(z + r, NZ)
        return remote(info_out.at[to], info_in.at[z], inf_send.at[r], inf_recv.at[r], at_z(to))

    def info_start(r, _):
        info_copy(r).start()
        return 0

    lax.fori_loop(1, NZ, info_start, 0)

    def kv_copy(h):
        return remote(KV.at[yh, h], KV.at[yh, h], kv_send.at[h], kv_recv.at[h], y_mate)

    for h in range(2):
        acc[...] = jnp.zeros_like(acc)

        def piece(k, _):
            if h == 0:
                x_load(k).wait()
            w_load(h, k).wait()
            rows = pl.ds(pl.multiple_of(k * depth, depth), depth)
            acc[...] += dot(X[k], W[rows, h * 256 : h * 256 + 256], NN)
            return 0

        lax.fori_loop(0, KC, piece, 0)
        KV[yh, h] = acc[...].astype(BF)
        kv_copy(h).start()

    def kv_wait(h):
        pltpu.make_async_remote_copy(
            src_ref=KV.at[1 - yh, h], dst_ref=KV.at[1 - yh, h], send_sem=kv_send.at[h],
            recv_sem=kv_recv.at[h], device_id=y_mate, device_id_type=pl.DeviceIdType.MESH,
        ).wait_recv()

    def info_wait(r, _):
        info_copy(r).wait_recv()
        return 0

    lax.fori_loop(1, NZ, info_wait, 0)
    for h in range(2):
        kv_wait(h)

    def chosen(j, h):
        out = []
        for w in range(2):
            f = info_in[j, 2 + w : 3 + w, :] + jnp.zeros((CL, 256), F32)
            one, zero = f.astype(BF), (1.0 - f).astype(BF)
            out.append(KV[w, h, 0:CL, :] * zero + KV[w, h, CL : 2 * CL, :] * one)
        return jnp.concatenate(out, axis=0)

    def st_copy(j):
        r = lax.rem(j - z + NZ, NZ)
        return remote(st_out.at[j], st_in.at[z], st_send.at[r], st_recv.at[r], at_z(j))

    def att1(j):
        for h in range(2):
            kv = chosen(j, h)
            cols = slice(h * HS, h * HS + HS)
            sc = dot(kv[:, :HS], G[j, 0, :, cols], NT) * scaling
            sc = jnp.concatenate(
                [
                    jnp.where(info_in[j, w : w + 1, :] > 0.0, sc[w * CL : w * CL + CL], NEG)
                    for w in range(2)
                ],
                axis=0,
            )
            top = jnp.max(sc, axis=0, keepdims=True)
            e = jnp.exp(sc - top)
            dp = dot(kv[:, HS:], G[j, 1, :, cols], NT)
            E[j, h] = e
            DP[j, h] = dp
            st_out[j, 3 * h : 3 * h + 1, :] = top
            st_out[j, 3 * h + 1 : 3 * h + 2, :] = jnp.sum(e, axis=0, keepdims=True)
            st_out[j, 3 * h + 2 : 3 * h + 3, :] = jnp.sum(e * dp, axis=0, keepdims=True)
        st_out[j, 6:8, :] = jnp.zeros((2, 256), F32)

    def hop(t, _):
        @pl.when(t > 0)
        def _():
            ag(0, 0, t - 1).wait_recv()
            ag(1, 1, t - 1).wait_recv()

            @pl.when(t < 4)
            def _():
                ag(0, 0, t).start()
                ag(1, 1, t).start()
                ag(0, 1, t - 1).wait_recv()
                ag(1, 0, t - 1).wait_recv()

                @pl.when(t < 3)
                def _():
                    ag(0, 1, t).start()
                    ag(1, 0, t).start()

        def side(i, _):
            j = lax.rem(z + NZ - t + 2 * i * t, NZ)
            att1(j)

            @pl.when(t > 0)
            def _():
                st_copy(j).start()

            return 0

        lax.fori_loop(0, jnp.where((t == 0) | (t == 4), 1, 2), side, 0)
        return 0

    lax.fori_loop(0, 5, hop, 0)

    st_in[z] = st_out[z]

    def st_wait(r, _):
        src = lax.rem(z + NZ - r, NZ)
        remote(st_out.at[src], st_in.at[src], st_send.at[r], st_recv.at[r], at_z(src)).wait_recv()
        return 0

    lax.fori_loop(1, NZ, st_wait, 0)
    for h in range(2):
        tops = [st_in[i, 3 * h : 3 * h + 1, :] for i in range(NZ)]
        top = functools.reduce(jnp.maximum, tops)
        total = jnp.zeros((1, 256), F32)
        dots = jnp.zeros((1, 256), F32)
        for i in range(NZ):
            f = jnp.exp(tops[i] - top)
            total += f * st_in[i, 3 * h + 1 : 3 * h + 2, :]
            dots += f * st_in[i, 3 * h + 2 : 3 * h + 3, :]
        res_out[3 * h : 3 * h + 1, :] = top
        res_out[3 * h + 1 : 3 * h + 2, :] = 1.0 / total
        res_out[3 * h + 2 : 3 * h + 3, :] = dots / total
    res_out[6:8, :] = jnp.zeros((2, 256), F32)
    res_in[z] = res_out[...]

    def res_copy(r):
        return remote(res_out, res_in.at[z], rs_send.at[r], rs_recv.at[r], at_z(lax.rem(z + r, NZ)))

    def res_start(r, _):
        res_copy(r).start()
        return 0

    lax.fori_loop(1, NZ, res_start, 0)
    GR[...] = jnp.zeros_like(GR)

    def at_copy(j):
        r = lax.rem(j - z + NZ, NZ)
        return remote(at_out.at[j], at_in.at[z], at_send.at[r], at_recv.at[r], at_z(j))

    def att2(r, _):
        j = lax.rem(z + NZ - r, NZ)

        @pl.when(r > 0)
        def _():
            remote(res_out, res_in.at[j], rs_send.at[r], rs_recv.at[r], at_z(j)).wait_recv()

        for h in range(2):
            cols = slice(h * HS, h * HS + HS)
            f = jnp.exp(st_out[j, 3 * h : 3 * h + 1, :] - res_in[j, 3 * h : 3 * h + 1, :])
            p = E[j, h] * (f * res_in[j, 3 * h + 1 : 3 * h + 2, :])
            rounded = p.astype(BF)
            ds = (p * (DP[j, h] - res_in[j, 3 * h + 2 : 3 * h + 3, :])).astype(BF)
            kg = dot(ds, G[j, 0, :, cols], NN) * scaling
            vg = dot(rounded, G[j, 1, :, cols], NN)
            part = jnp.concatenate([kg, vg], axis=1)
            for w in range(2):
                one = info_in[j, 2 + w : 3 + w, :]
                mine = part[w * CL : w * CL + CL]
                GR[w, 0:CL, h * 256 : h * 256 + 256] += mine * (1.0 - one)
                GR[w, CL : 2 * CL, h * 256 : h * 256 + 256] += mine * one
            values = chosen(j, h)[:, HS:]
            at_out[j, cols, :] = dot(values, rounded, TN).astype(BF)

        @pl.when(r > 0)
        def _():
            at_copy(j).start()

        return 0

    lax.fori_loop(0, NZ, att2, 0)
    at_in[z] = at_out[z]

    yg_out[...] = GR[1 - yh].astype(BF)
    yg = remote(yg_out, yg_in, yg_send, yg_recv, y_mate)
    yg.start()
    yg.wait_recv()
    kvg[...] = (GR[yh] + yg_in[...].astype(F32)).astype(BF)

    def w_rows(i, core):
        e = ((i // 2) * 2 + core) * 2 + i % 2
        return W[pl.ds(pl.multiple_of(e * 512, 512), 512), :]

    def cs_copy(i):
        return remote(cs_out.at[i], cs_in.at[i], cs_send.at[i], cs_recv.at[i], core_mate)

    def to_core(i, _):
        cs_out[i] = dot(kvg[...], w_rows(i, 1 - c), NT).astype(BF)
        cs_copy(i).start()
        return 0

    lax.fori_loop(0, 8, to_core, 0)

    def own_core(i, _):
        own = dot(kvg[...], w_rows(i, c), NT)
        cs_copy(i).wait_recv()
        R[i // 2, i % 2] = (own + cs_in[i].astype(F32)).astype(BF)
        return 0

    lax.fori_loop(0, 8, own_core, 0)

    two, nxt, prv = lax.rem(x + 2, NX), lax.rem(x + 1, NX), lax.rem(x + 3, NX)

    def xsum(src, tmp, into, ssem, rsem):
        def at(i, half):
            return src(i, slice(half * 256, half * 256 + 256))

        firsts = [
            remote(at(two, 0), into.at[0], ssem.at[0], rsem.at[0], x_right),
            remote(at(two, 1), into.at[1], ssem.at[1], rsem.at[1], x_left),
            remote(at(nxt, 1), into.at[2], ssem.at[2], rsem.at[2], x_right),
            remote(at(prv, 0), into.at[3], ssem.at[3], rsem.at[3], x_left),
        ]
        seconds = [
            remote(tmp.at[0], into.at[4], ssem.at[4], rsem.at[4], x_right),
            remote(tmp.at[1], into.at[5], ssem.at[5], rsem.at[5], x_left),
        ]

        def relay():
            for i, (to, half) in enumerate([(nxt, 0), (prv, 1)]):
                firsts[i].wait_recv()
                tmp[i] = (at(to, half)[...].astype(F32) + into[i].astype(F32)).astype(BF)
                seconds[i].start()

        def finish():
            firsts[2].wait_recv()
            firsts[3].wait_recv()
            seconds[0].wait_recv()
            seconds[1].wait_recv()
            halves = []
            for half, got in [(0, (4, 3)), (1, (2, 5))]:
                v = at(x, half)[...].astype(F32)
                for g in got:
                    v += into[g].astype(F32)
                halves.append(v)
            return halves

        def start():
            for cp in firsts:
                cp.start()

        def drain():
            for cp in firsts + seconds:
                cp.wait_send()

        return start, relay, finish, drain

    a_start, a_relay, a_finish, a_drain = xsum(
        lambda i, cols: R.at[i, :, 0:CL, cols], ax_tmp, ax_in, ax_send, ax_recv
    )
    b_start, b_relay, b_finish, b_drain = xsum(
        lambda i, cols: RB.at[i, :, cols], bx_tmp, bx_in, bx_send, bx_recv
    )
    by = remote(R.at[:, 1 - m, CL : 2 * CL, :], by_in, by_send, by_recv, m_mate)
    a_start()
    by.start()
    a_relay()
    by.wait_recv()

    def add_b(i, _):
        RB[i] = (R[i, m, CL : 2 * CL, :].astype(F32) + by_in[i].astype(F32)).astype(BF)
        return 0

    lax.fori_loop(0, NX, add_b, 0)
    b_start()
    fa = a_finish()
    for half in range(2):
        cols = slice(half * 256, half * 256 + 256)
        ay_out[:, :, cols] = fa[half].astype(BF)
    ay = remote(ay_out.at[1 - m], ay_in, ay_send, ay_recv, m_mate)
    ay.start()
    b_relay()

    def at_wait(r, _):
        src = lax.rem(z + NZ - r, NZ)
        remote(at_out.at[src], at_in.at[src], at_send.at[r], at_recv.at[r], at_z(src)).wait_recv()
        return 0

    lax.fori_loop(1, NZ, at_wait, 0)
    total = at_in[0].astype(F32)
    for i in range(1, NZ):
        total += at_in[i].astype(F32)
    att_ref[...] = total.T.astype(BF)

    fb = b_finish()
    for half in range(2):
        cols = slice(half * 256, half * 256 + 256)
        nbr_ref[CL : 2 * CL, cols] = fb[half].astype(BF)
    ay.wait_recv()
    nbr_ref[0:CL, :] = (ay_out[m].astype(F32) + ay_in[...].astype(F32)).astype(BF)

    for direction in range(2):
        for arr in range(2):
            for t in range(4 if direction == arr else 3):
                ag(direction, arr, t).wait_send()
    for h in range(2):
        kv_copy(h).wait_send()

    def sent(r, _):
        j = lax.rem(z + r, NZ)
        info_copy(r).wait_send()
        st_copy(j).wait_send()
        res_copy(r).wait_send()
        at_copy(j).wait_send()
        return 0

    lax.fori_loop(1, NZ, sent, 0)
    yg.wait_send()

    def cs_sent(i, _):
        cs_copy(i).wait_send()
        return 0

    lax.fori_loop(0, 8, cs_sent, 0)
    by.wait_send()
    ay.wait_send()
    a_drain()
    b_drain()


def on_device(nbr_states, kv_weight, queries, out_grad, citations):
    width = kv_weight.shape[0]
    weight = kv_weight.reshape(width, 2, 2, HS).transpose(0, 2, 1, 3).reshape(width, 4 * HS)
    V, D = pltpu.VMEM, pltpu.SemaphoreType.DMA
    scratch = [
        V((KC, 256, width // KC), BF),
        V((width, 512), BF),
        V((256, 256), F32),
        V((NZ, 2, 256, 256), BF),
        V((2, 2, 256, 256), BF),
        V((NZ, 8, 256), F32),
        V((NZ, 8, 256), F32),
        V((NZ, 2, 256, 256), F32),
        V((NZ, 2, 256, 256), F32),
        V((NZ, 8, 256), F32),
        V((NZ, 8, 256), F32),
        V((8, 256), F32),
        V((NZ, 8, 256), F32),
        V((NZ, 256, 256), BF),
        V((NZ, 256, 256), BF),
        V((2, 256, 512), F32),
        V((256, 512), BF),
        V((256, 512), BF),
        V((256, 512), BF),
        V((8, 256, 512), BF),
        V((8, 256, 512), BF),
        V((NX, 2, 256, 512), BF),
        V((NX, CL, 512), BF),
        V((NX, CL, 512), BF),
        V((6, 2, CL, 256), BF),
        V((2, 2, CL, 256), BF),
        V((6, CL, 256), BF),
        V((2, CL, 256), BF),
        V((2, CL, 512), BF),
        V((CL, 512), BF),
        D((3, KC)),
        D((2, 2, 4)), D((2, 2, 4)),
        D((2,)), D((2,)),
        D((NZ,)), D((NZ,)),
        D((NZ,)), D((NZ,)),
        D((NZ,)), D((NZ,)),
        D((NZ,)), D((NZ,)),
        D, D,
        D((8,)), D((8,)),
        D, D,
        D((6,)), D((6,)),
        D((6,)), D((6,)),
        D, D,
    ]
    vmem = pl.BlockSpec(memory_space=pltpu.VMEM)
    hbm = pl.BlockSpec(memory_space=pl.ANY)
    return pl.pallas_call(
        kernel,
        out_shape=(
            jax.ShapeDtypeStruct((256, 256), BF),
            jax.ShapeDtypeStruct((256, 512), BF),
        ),
        in_specs=[pl.BlockSpec(memory_space=pltpu.SMEM), vmem, vmem, hbm, hbm],
        out_specs=(vmem, vmem),
        scratch_shapes=scratch,
        compiler_params=pltpu.CompilerParams(
            collective_id=0, has_side_effects=True, vmem_limit_bytes=56 * 2**20
        ),
        cost_estimate=pl.CostEstimate(
            flops=6 * 10**9, bytes_accessed=13 * 2**20, transcendentals=2 * 10**6
        ),
    )(citations, queries, out_grad, nbr_states, weight)


def solution(mesh):
    heads = ("section", "mp")
    return jax.shard_map(
        on_device,
        mesh=mesh,
        in_specs=(
            P("dp", None),
            P(None, None, heads),
            P("dp", heads),
            P("dp", heads),
            P("dp", None),
        ),
        out_specs=(P("dp", heads), P("dp", heads)),
        check_vma=False,
    )
```

time: 574 us -> 107 us (0.19)
  the two profiles are of different devices: /device:TPU:1 before, /device:TPU:8 now
where the time goes in v1:
time: 107 us
  Pallas kernels  88.6 us (83%)
  local copies, waits for them, and re-layouts  17.7 us (17%)
    pallas_call x1, Pallas kernels, on_device(): pl.pallas_call(kernel, out_shape=(jax.ShapeDtypeStruct((256, 256), BF), j...  88.6 us
    reshape x1, local copies, waits for them, and re-layouts, on_device(): kv_weight.reshape(width, 2, 2, HS).transpose(0, 2, 1, 3)  13.1 us
    unnamed x3, local copies, waits for them, and re-layouts  4.57 us

profile of v1, /device:TPU:8, one launch (start us, length us, event | category | flops | bytes accessed | tf_op | source)
XLA Modules:
  0.0 107.0 jit_solution(12927953895892909105)
XLA Ops:
  0.6 1.3 %copy.8.cit_ref = s32[4,2]{1,0:T(4,128)} copy(s32[4,2]{0,1:T(2,128)} %param.9) | data formatting | bytes 64 | tf_op args[4]
  2.0 13.1 %reshape.11.w_hbm = bf16[8192,512]{1,0:T(8,128)(2,1)} reshape(bf16[8192,2,2,128]{3,2,1,0:T(2,128)(2,1)} %bitcast.3) | data formatting | bytes 16777216 | tf_op jit(solution)/shard_map/reshape | solution.py:454
  15.1 88.6 %shard_map.68 = (bf16[256,256]{1,0:T(8,128)(2,1)}, bf16[256,512]{1,0:T(8,128)(2,1)}) custom-call(s32[4,2]{1,0:T(4,128)} %copy.8.cit_ref, bf16[256,256]{1,0:T(8,128)(2,1)} %q_ref.1, bf16[256,256]{1,0:T(8,128)(2,1)} %g_ref.1, bf16[256,8192]{1,0:T(8,128)(2,1)} %x_hbm.1, bf16[8192,512]{1,0:T(8,128)(2,1)} %reshape.11.w_hbm), custom_call_target="tpu_custom_call" | custom-call | flops 6000000000 | bytes 13631488 | tf_op jit(solution)/shard_map/pallas_call | solution.py:503
  103.7 1.6 %copy.11 = bf16[256,256]{1,0:T(8,128)(2,1)} copy(bf16[256,256]{1,0:T(8,128)(2,1)} %get-tuple-element.4) | data formatting | bytes 262144
  105.3 1.7 %copy.12 = bf16[256,512]{1,0:T(8,128)(2,1)} copy(bf16[256,512]{1,0:T(8,128)(2,1)} %get-tuple-element.5) | data formatting | bytes 524288

commit v2 on v1

--- a/solution.py
+++ b/solution.py
@@ -13,6 +13,7 @@
 NZ = 8
 NX = 4
 KC = 8
+ROWS_A = 144
 NEG = -1e30
 BF = jnp.bfloat16
 F32 = jnp.float32
@@ -27,9 +28,9 @@
 
 def kernel(
     cit_ref, q_ref, g_ref, x_hbm, w_hbm, att_ref, nbr_ref,
-    X, W, acc, G, KV, info_out, info_in, E, DP, st_out, st_in, res_out, res_in,
+    X, W32, W, acc, G, KV, info_out, info_in, E, DP, st_out, st_in, res_out, res_in,
     at_out, at_in, GR, yg_out, yg_in, kvg, cs_out, cs_in, R, by_in, RB,
-    ax_in, ax_tmp, bx_in, bx_tmp, ay_out, ay_in,
+    ax_in, ax_tmp, bx_in, bx_tmp, ay_out, ay_in, PM,
     ld_sem, ag_send, ag_recv, kv_send, kv_recv, inf_send, inf_recv, st_send, st_recv,
     rs_send, rs_recv, at_send, at_recv, yg_send, yg_recv, cs_send, cs_recv,
     by_send, by_recv, ax_send, ax_recv, bx_send, bx_recv, ay_send, ay_recv,
@@ -57,27 +58,20 @@
 
     def x_load(k):
         return pltpu.make_async_copy(
-            x_hbm.at[:, pl.ds(pl.multiple_of(k * depth, depth), depth)], X.at[k], ld_sem.at[2, k]
+            x_hbm.at[:, pl.ds(pl.multiple_of(k * depth, depth), depth)], X.at[k], ld_sem.at[1, k]
         )
 
-    def w_load(h, k):
-        rows = pl.ds(pl.multiple_of(k * depth, depth), depth)
+    def w_load(k):
         return pltpu.make_async_copy(
-            w_hbm.at[rows, pl.ds(h * 256, 256)], W.at[rows, pl.ds(h * 256, 256)], ld_sem.at[h, k]
+            w_hbm.at[pl.ds(pl.multiple_of(k * 4 * depth, depth), 4 * depth), :], W32.at[k], ld_sem.at[0, k]
         )
 
     def start_loads(k, _):
+        w_load(k).start()
         x_load(k).start()
-        w_load(0, k).start()
         return 0
 
     lax.fori_loop(0, KC, start_loads, 0)
-
-    def start_loads_1(k, _):
-        w_load(1, k).start()
-        return 0
-
-    lax.fori_loop(0, KC, start_loads_1, 0)
 
     barrier = pltpu.get_barrier_semaphore()
     for dev in [at_z(lax.rem(z + r, NZ)) for r in range(1, NZ)] + [
@@ -93,7 +87,7 @@
     for k in range(2):
         v = jnp.zeros((16, 256), jnp.int32)
         for b in range(4):
-            v = jnp.where(lane == b, cit_ref[b, k], v)
+            v = jnp.where(lane == b, cit_ref[k, b], v)
         ids.append(v)
     second = (ids[0] == owner * 2 + 1) | (ids[1] == owner * 2 + 1)
     first = (ids[0] == owner * 2) | (ids[1] == owner * 2)
@@ -133,22 +127,47 @@
 
     lax.fori_loop(1, NZ, info_start, 0)
 
+    def relay(t):
+        for direction in range(2):
+            for arr in range(2):
+                ag(direction, arr, t - 1).wait_recv()
+                if t < 3 or direction == arr:
+                    ag(direction, arr, t).start()
+
+    out_row = lax.broadcasted_iota(jnp.int32, (256, 256), 0)
+    in_row = lax.broadcasted_iota(jnp.int32, (256, 256), 1)
+    PM[...] = jnp.where(in_row == (out_row % 64) * 4 + out_row // 64, 1.0, 0.0).astype(BF)
+
+    def piece(k):
+        w_load(k).wait()
+
+        def sort(i, _):
+            for u in range(4):
+                b = i * 4 + u
+                got = dot(PM[...], W32[k, pl.ds(pl.multiple_of(b * 256, 256), 256), :], NN).astype(BF)
+                rows = pl.ds(pl.multiple_of(k * depth + b * 64, 64), 64)
+                for n in range(4):
+                    W[rows, n * HS : n * HS + HS] = got[n * 64 : n * 64 + 64]
+            return 0
+
+        lax.fori_loop(0, depth // 256, sort, 0)
+        x_load(k).wait()
+        rows = pl.ds(pl.multiple_of(k * depth, depth), depth)
+        acc[...] += dot(X[k], W[rows, :], NN)
+
+    def piece_loop(k, _):
+        piece(k)
+        return 0
+
     def kv_copy(h):
         return remote(KV.at[yh, h], KV.at[yh, h], kv_send.at[h], kv_recv.at[h], y_mate)
 
+    acc[...] = jnp.zeros_like(acc)
+    lax.fori_loop(0, KC - 2, piece_loop, 0)
+    relay(1)
+    lax.fori_loop(KC - 2, KC, piece_loop, 0)
     for h in range(2):
-        acc[...] = jnp.zeros_like(acc)
-
-        def piece(k, _):
-            if h == 0:
-                x_load(k).wait()
-            w_load(h, k).wait()
-            rows = pl.ds(pl.multiple_of(k * depth, depth), depth)
-            acc[...] += dot(X[k], W[rows, h * 256 : h * 256 + 256], NN)
-            return 0
-
-        lax.fori_loop(0, KC, piece, 0)
-        KV[yh, h] = acc[...].astype(BF)
+        KV[yh, h] = acc[:, h * 256 : h * 256 + 256].astype(BF)
         kv_copy(h).start()
 
     def kv_wait(h):
@@ -161,6 +180,7 @@
         info_copy(r).wait_recv()
         return 0
 
+    relay(2)
     lax.fori_loop(1, NZ, info_wait, 0)
     for h in range(2):
         kv_wait(h)
@@ -199,38 +219,23 @@
             st_out[j, 3 * h + 2 : 3 * h + 3, :] = jnp.sum(e * dp, axis=0, keepdims=True)
         st_out[j, 6:8, :] = jnp.zeros((2, 256), F32)
 
-    def hop(t, _):
-        @pl.when(t > 0)
-        def _():
-            ag(0, 0, t - 1).wait_recv()
-            ag(1, 1, t - 1).wait_recv()
-
-            @pl.when(t < 4)
-            def _():
-                ag(0, 0, t).start()
-                ag(1, 1, t).start()
-                ag(0, 1, t - 1).wait_recv()
-                ag(1, 0, t - 1).wait_recv()
-
-                @pl.when(t < 3)
-                def _():
-                    ag(0, 1, t).start()
-                    ag(1, 0, t).start()
-
+    def both(t):
         def side(i, _):
             j = lax.rem(z + NZ - t + 2 * i * t, NZ)
             att1(j)
-
-            @pl.when(t > 0)
-            def _():
-                st_copy(j).start()
-
+            st_copy(j).start()
             return 0
 
-        lax.fori_loop(0, jnp.where((t == 0) | (t == 4), 1, 2), side, 0)
-        return 0
-
-    lax.fori_loop(0, 5, hop, 0)
+        lax.fori_loop(0, 1 if t == 4 else 2, side, 0)
+
+    att1(z)
+    both(1)
+    relay(3)
+    both(2)
+    both(3)
+    ag(0, 0, 3).wait_recv()
+    ag(1, 1, 3).wait_recv()
+    both(4)
 
     st_in[z] = st_out[z]
 
@@ -377,19 +382,19 @@
         return start, relay, finish, drain
 
     a_start, a_relay, a_finish, a_drain = xsum(
-        lambda i, cols: R.at[i, :, 0:CL, cols], ax_tmp, ax_in, ax_send, ax_recv
+        lambda i, cols: R.at[i, :, 0:ROWS_A, cols], ax_tmp, ax_in, ax_send, ax_recv
     )
     b_start, b_relay, b_finish, b_drain = xsum(
         lambda i, cols: RB.at[i, :, cols], bx_tmp, bx_in, bx_send, bx_recv
     )
-    by = remote(R.at[:, 1 - m, CL : 2 * CL, :], by_in, by_send, by_recv, m_mate)
+    by = remote(R.at[:, 1 - m, ROWS_A:256, :], by_in, by_send, by_recv, m_mate)
     a_start()
     by.start()
     a_relay()
     by.wait_recv()
 
     def add_b(i, _):
-        RB[i] = (R[i, m, CL : 2 * CL, :].astype(F32) + by_in[i].astype(F32)).astype(BF)
+        RB[i] = (R[i, m, ROWS_A:256, :].astype(F32) + by_in[i].astype(F32)).astype(BF)
         return 0
 
     lax.fori_loop(0, NX, add_b, 0)
@@ -416,9 +421,9 @@
     fb = b_finish()
     for half in range(2):
         cols = slice(half * 256, half * 256 + 256)
-        nbr_ref[CL : 2 * CL, cols] = fb[half].astype(BF)
+        nbr_ref[ROWS_A:256, cols] = fb[half].astype(BF)
     ay.wait_recv()
-    nbr_ref[0:CL, :] = (ay_out[m].astype(F32) + ay_in[...].astype(F32)).astype(BF)
+    nbr_ref[0:ROWS_A, :] = (ay_out[m].astype(F32) + ay_in[...].astype(F32)).astype(BF)
 
     for direction in range(2):
         for arr in range(2):
@@ -451,12 +456,14 @@
 
 def on_device(nbr_states, kv_weight, queries, out_grad, citations):
     width = kv_weight.shape[0]
-    weight = kv_weight.reshape(width, 2, 2, HS).transpose(0, 2, 1, 3).reshape(width, 4 * HS)
+    rest = 256 - ROWS_A
+    weight = kv_weight.reshape(width, 2, 2, HS).transpose(0, 2, 1, 3).reshape(width * 4, HS)
     V, D = pltpu.VMEM, pltpu.SemaphoreType.DMA
     scratch = [
         V((KC, 256, width // KC), BF),
+        V((KC, width * 4 // KC, HS), BF),
         V((width, 512), BF),
-        V((256, 256), F32),
+        V((256, 512), F32),
         V((NZ, 2, 256, 256), BF),
         V((2, 2, 256, 256), BF),
         V((NZ, 8, 256), F32),
@@ -476,15 +483,16 @@
         V((8, 256, 512), BF),
         V((8, 256, 512), BF),
         V((NX, 2, 256, 512), BF),
-        V((NX, CL, 512), BF),
-        V((NX, CL, 512), BF),
-        V((6, 2, CL, 256), BF),
-        V((2, 2, CL, 256), BF),
-        V((6, CL, 256), BF),
-        V((2, CL, 256), BF),
-        V((2, CL, 512), BF),
-        V((CL, 512), BF),
-        D((3, KC)),
+        V((NX, rest, 512), BF),
+        V((NX, rest, 512), BF),
+        V((6, 2, ROWS_A, 256), BF),
+        V((2, 2, ROWS_A, 256), BF),
+        V((6, rest, 256), BF),
+        V((2, rest, 256), BF),
+        V((2, ROWS_A, 512), BF),
+        V((ROWS_A, 512), BF),
+        V((256, 256), BF),
+        D((2, KC)),
         D((2, 2, 4)), D((2, 2, 4)),
         D((2,)), D((2,)),
         D((NZ,)), D((NZ,)),
@@ -515,7 +523,7 @@
         cost_estimate=pl.CostEstimate(
             flops=6 * 10**9, bytes_accessed=13 * 2**20, transcendentals=2 * 10**6
         ),
-    )(citations, queries, out_grad, nbr_states, weight)
+    )(citations.T, queries, out_grad, nbr_states, weight)
 
 
 def solution(mesh):

time: 107 us -> 90 us (0.84)
  the two profiles are of different devices: /device:TPU:8 before, /device:TPU:1 now
where the time goes in v2:
time: 90 us; the launch traced here: 88.4 us
  Pallas kernels  84.6 us (94%)
  local copies, waits for them, and re-layouts  3.24 us (4%)
    pallas_call x1, Pallas kernels, on_device(): pl.pallas_call(kernel, out_shape=(jax.ShapeDtypeStruct((256, 256), BF), j...  84.6 us
    unnamed x2, local copies, waits for them, and re-layouts  3.24 us

profile of v2, /device:TPU:1, one launch (start us, length us, event | category | flops | bytes accessed | tf_op | source)
XLA Modules:
  0.0 88.4 jit_solution(15189220382361546303)
XLA Ops:
  0.6 84.6 %shard_map.68 = (bf16[256,256]{1,0:T(8,128)(2,1)}, bf16[256,512]{1,0:T(8,128)(2,1)}) custom-call(s32[2,4]{1,0:T(2,128)} %bitcast.7, bf16[256,256]{1,0:T(8,128)(2,1)} %q_ref.1, bf16[256,256]{1,0:T(8,128)(2,1)} %g_ref.1, bf16[256,8192]{1,0:T(8,128)(2,1)} %x_hbm.1, bf16[32768,128]{1,0:T(8,128)(2,1)} %bitcast.6), custom_call_target="tpu_custom_call" | custom-call | flops 6000000000 | bytes 13631488 | tf_op jit(solution)/shard_map/pallas_call | solution.py:511
  85.2 1.6 %copy.10 = bf16[256,256]{1,0:T(8,128)(2,1)} copy(bf16[256,256]{1,0:T(8,128)(2,1)} %get-tuple-element.4) | data formatting | bytes 262144
  86.8 1.7 %copy.11 = bf16[256,512]{1,0:T(8,128)(2,1)} copy(bf16[256,512]{1,0:T(8,128)(2,1)} %get-tuple-element.5) | data formatting | bytes 524288

commit v3 on v2

--- a/solution.py
+++ b/solution.py
@@ -103,19 +103,17 @@
     info_in[z] = info_out[z]
     pl.semaphore_wait(barrier, 12)
 
-    def ag(direction, arr, t):
+    def ag(direction, u, t):
         if direction == 0:
-            home, to = lax.rem(z - t + NZ, NZ), lax.rem(z + 1, NZ)
+            home, to, arr = lax.rem(z - t + NZ, NZ), lax.rem(z + 1, NZ), u // 2
         else:
-            home, to = lax.rem(z + t, NZ), lax.rem(z + NZ - 1, NZ)
-        return remote(
-            G.at[home, arr], G.at[home, arr],
-            ag_send.at[direction, arr, t], ag_recv.at[direction, arr, t], at_z(to),
-        )
-
-    for direction in range(2):
-        for arr in range(2):
-            ag(direction, arr, 0).start()
+            home, to, arr = lax.rem(z + t, NZ), lax.rem(z + NZ - 1, NZ), 1 - u // 2
+        piece = G.at[home, arr, pl.ds(pl.multiple_of((u % 2) * 128, 128), 128)]
+        return remote(piece, piece, ag_send.at[direction, u, t], ag_recv.at[direction, u, t], at_z(to))
+
+    for u in range(4):
+        for direction in range(2):
+            ag(direction, u, 0).start()
 
     def info_copy(r):
         to = lax.rem(z + r, NZ)
@@ -127,18 +125,20 @@
 
     lax.fori_loop(1, NZ, info_start, 0)
 
-    def relay(t):
+    def relay(t, u):
         for direction in range(2):
-            for arr in range(2):
-                ag(direction, arr, t - 1).wait_recv()
-                if t < 3 or direction == arr:
-                    ag(direction, arr, t).start()
+            ag(direction, u, t - 1).wait_recv()
+            ag(direction, u, t).start()
+
+    def arrived(t, u):
+        for direction in range(2):
+            ag(direction, u, t).wait_recv()
 
     out_row = lax.broadcasted_iota(jnp.int32, (256, 256), 0)
     in_row = lax.broadcasted_iota(jnp.int32, (256, 256), 1)
     PM[...] = jnp.where(in_row == (out_row % 64) * 4 + out_row // 64, 1.0, 0.0).astype(BF)
 
-    def piece(k):
+    def piece(k, _):
         w_load(k).wait()
 
         def sort(i, _):
@@ -153,21 +153,26 @@
         lax.fori_loop(0, depth // 256, sort, 0)
         x_load(k).wait()
         rows = pl.ds(pl.multiple_of(k * depth, depth), depth)
-        acc[...] += dot(X[k], W[rows, :], NN)
-
-    def piece_loop(k, _):
-        piece(k)
+        acc[...] += dot(X[k], W[rows, 0:256], NN)
+
+        @pl.when(k >= 2)
+        def _():
+            relay(1 + (k - 2) // 4, (k - 2) % 4)
+
+        return 0
+
+    def piece_1(k, _):
+        rows = pl.ds(pl.multiple_of(k * depth, depth), depth)
+        acc[...] += dot(X[k], W[rows, 256:512], NN)
         return 0
 
     def kv_copy(h):
         return remote(KV.at[yh, h], KV.at[yh, h], kv_send.at[h], kv_recv.at[h], y_mate)
 
-    acc[...] = jnp.zeros_like(acc)
-    lax.fori_loop(0, KC - 2, piece_loop, 0)
-    relay(1)
-    lax.fori_loop(KC - 2, KC, piece_loop, 0)
-    for h in range(2):
-        KV[yh, h] = acc[:, h * 256 : h * 256 + 256].astype(BF)
+    for h, body in enumerate([piece, piece_1]):
+        acc[...] = jnp.zeros_like(acc)
+        lax.fori_loop(0, KC, body, 0)
+        KV[yh, h] = acc[...].astype(BF)
         kv_copy(h).start()
 
     def kv_wait(h):
@@ -180,8 +185,10 @@
         info_copy(r).wait_recv()
         return 0
 
-    relay(2)
+    relay(2, 2)
+    relay(2, 3)
     lax.fori_loop(1, NZ, info_wait, 0)
+    relay(3, 0)
     for h in range(2):
         kv_wait(h)
 
@@ -228,13 +235,15 @@
 
         lax.fori_loop(0, 1 if t == 4 else 2, side, 0)
 
+    relay(3, 1)
     att1(z)
     both(1)
-    relay(3)
     both(2)
+    arrived(2, 2)
+    arrived(2, 3)
     both(3)
-    ag(0, 0, 3).wait_recv()
-    ag(1, 1, 3).wait_recv()
+    arrived(3, 0)
+    arrived(3, 1)
     both(4)
 
     st_in[z] = st_out[z]
@@ -297,11 +306,6 @@
                 GR[w, CL : 2 * CL, h * 256 : h * 256 + 256] += mine * one
             values = chosen(j, h)[:, HS:]
             at_out[j, cols, :] = dot(values, rounded, TN).astype(BF)
-
-        @pl.when(r > 0)
-        def _():
-            at_copy(j).start()
-
         return 0
 
     lax.fori_loop(0, NZ, att2, 0)
@@ -310,52 +314,69 @@
     yg_out[...] = GR[1 - yh].astype(BF)
     yg = remote(yg_out, yg_in, yg_send, yg_recv, y_mate)
     yg.start()
+
+    def at_start(r, _):
+        at_copy(lax.rem(z + r, NZ)).start()
+        return 0
+
+    lax.fori_loop(1, NZ, at_start, 0)
     yg.wait_recv()
     kvg[...] = (GR[yh] + yg_in[...].astype(F32)).astype(BF)
 
-    def w_rows(i, core):
-        e = ((i // 2) * 2 + core) * 2 + i % 2
-        return W[pl.ds(pl.multiple_of(e * 512, 512), 512), :]
-
-    def cs_copy(i):
-        return remote(cs_out.at[i], cs_in.at[i], cs_send.at[i], cs_recv.at[i], core_mate)
-
-    def to_core(i, _):
-        cs_out[i] = dot(kvg[...], w_rows(i, 1 - c), NT).astype(BF)
-        cs_copy(i).start()
-        return 0
-
-    lax.fori_loop(0, 8, to_core, 0)
-
-    def own_core(i, _):
-        own = dot(kvg[...], w_rows(i, c), NT)
-        cs_copy(i).wait_recv()
-        R[i // 2, i % 2] = (own + cs_in[i].astype(F32)).astype(BF)
-        return 0
-
-    lax.fori_loop(0, 8, own_core, 0)
-
     two, nxt, prv = lax.rem(x + 2, NX), lax.rem(x + 1, NX), lax.rem(x + 3, NX)
+    order = [two, nxt, prv, x]
+
+    def product(n, core, yl):
+        e = (order[n] * 2 + core) * 2 + yl
+        return dot(kvg[...], W[pl.ds(pl.multiple_of(e * 512, 512), 512), :], NT)
+
+    def cs_copy(n, yl):
+        return remote(cs_out.at[n, yl], cs_in.at[n, yl], cs_send.at[n, yl], cs_recv.at[n, yl], core_mate)
+
+    def for_mate(n):
+        def one(yl, _):
+            cs_out[n, yl] = product(n, 1 - c, yl).astype(BF)
+            cs_copy(n, yl).start()
+            return 0
+
+        lax.fori_loop(0, 2, one, 0)
+
+    def by_copy(n):
+        return remote(R.at[n, 1 - m, ROWS_A:256, :], by_in.at[n], by_send.at[n], by_recv.at[n], m_mate)
+
+    def own(n):
+        def one(yl, _):
+            mine = product(n, c, yl)
+            cs_copy(n, yl).wait_recv()
+            R[n, yl] = (mine + cs_in[n, yl].astype(F32)).astype(BF)
+            return 0
+
+        lax.fori_loop(0, 2, one, 0)
+        by_copy(n).start()
 
     def xsum(src, tmp, into, ssem, rsem):
-        def at(i, half):
-            return src(i, slice(half * 256, half * 256 + 256))
+        def at(n, half):
+            return src(n, slice(half * 256, half * 256 + 256))
 
         firsts = [
-            remote(at(two, 0), into.at[0], ssem.at[0], rsem.at[0], x_right),
-            remote(at(two, 1), into.at[1], ssem.at[1], rsem.at[1], x_left),
-            remote(at(nxt, 1), into.at[2], ssem.at[2], rsem.at[2], x_right),
-            remote(at(prv, 0), into.at[3], ssem.at[3], rsem.at[3], x_left),
+            remote(at(0, 0), into.at[0], ssem.at[0], rsem.at[0], x_right),
+            remote(at(0, 1), into.at[1], ssem.at[1], rsem.at[1], x_left),
+            remote(at(1, 1), into.at[2], ssem.at[2], rsem.at[2], x_right),
+            remote(at(2, 0), into.at[3], ssem.at[3], rsem.at[3], x_left),
         ]
         seconds = [
             remote(tmp.at[0], into.at[4], ssem.at[4], rsem.at[4], x_right),
             remote(tmp.at[1], into.at[5], ssem.at[5], rsem.at[5], x_left),
         ]
 
+        def start(n):
+            for i in [(0, 1), (2,), (3,), ()][n]:
+                firsts[i].start()
+
         def relay():
-            for i, (to, half) in enumerate([(nxt, 0), (prv, 1)]):
+            for i in range(2):
                 firsts[i].wait_recv()
-                tmp[i] = (at(to, half)[...].astype(F32) + into[i].astype(F32)).astype(BF)
+                tmp[i] = (at(1 + i, i)[...].astype(F32) + into[i].astype(F32)).astype(BF)
                 seconds[i].start()
 
         def finish():
@@ -365,16 +386,12 @@
             seconds[1].wait_recv()
             halves = []
             for half, got in [(0, (4, 3)), (1, (2, 5))]:
-                v = at(x, half)[...].astype(F32)
+                v = at(3, half)[...].astype(F32)
                 for g in got:
                     v += into[g].astype(F32)
                 halves.append(v)
             return halves
 
-        def start():
-            for cp in firsts:
-                cp.start()
-
         def drain():
             for cp in firsts + seconds:
                 cp.wait_send()
@@ -382,23 +399,31 @@
         return start, relay, finish, drain
 
     a_start, a_relay, a_finish, a_drain = xsum(
-        lambda i, cols: R.at[i, :, 0:ROWS_A, cols], ax_tmp, ax_in, ax_send, ax_recv
+        lambda n, cols: R.at[n, :, 0:ROWS_A, cols], ax_tmp, ax_in, ax_send, ax_recv
     )
     b_start, b_relay, b_finish, b_drain = xsum(
-        lambda i, cols: RB.at[i, :, cols], bx_tmp, bx_in, bx_send, bx_recv
+        lambda n, cols: RB.at[n, :, cols], bx_tmp, bx_in, bx_send, bx_recv
     )
-    by = remote(R.at[:, 1 - m, ROWS_A:256, :], by_in, by_send, by_recv, m_mate)
-    a_start()
-    by.start()
+
+    def add_b(n):
+        by_copy(n).wait_recv()
+        RB[n] = (R[n, m, ROWS_A:256, :].astype(F32) + by_in[n].astype(F32)).astype(BF)
+        b_start(n)
+
+    for_mate(0)
+    for_mate(1)
+    own(0)
+    a_start(0)
+    for_mate(2)
+    own(1)
+    a_start(1)
+    for_mate(3)
+    own(2)
+    a_start(2)
     a_relay()
-    by.wait_recv()
-
-    def add_b(i, _):
-        RB[i] = (R[i, m, ROWS_A:256, :].astype(F32) + by_in[i].astype(F32)).astype(BF)
-        return 0
-
-    lax.fori_loop(0, NX, add_b, 0)
-    b_start()
+    own(3)
+    for n in range(NX):
+        add_b(n)
     fa = a_finish()
     for half in range(2):
         cols = slice(half * 256, half * 256 + 256)
@@ -426,9 +451,9 @@
     nbr_ref[0:ROWS_A, :] = (ay_out[m].astype(F32) + ay_in[...].astype(F32)).astype(BF)
 
     for direction in range(2):
-        for arr in range(2):
-            for t in range(4 if direction == arr else 3):
-                ag(direction, arr, t).wait_send()
+        for u in range(4):
+            for t in range(4 if u < 2 else 3):
+                ag(direction, u, t).wait_send()
     for h in range(2):
         kv_copy(h).wait_send()
 
@@ -443,12 +468,10 @@
     lax.fori_loop(1, NZ, sent, 0)
     yg.wait_send()
 
-    def cs_sent(i, _):
-        cs_copy(i).wait_send()
-        return 0
-
-    lax.fori_loop(0, 8, cs_sent, 0)
-    by.wait_send()
+    for n in range(NX):
+        for yl in range(2):
+            cs_copy(n, yl).wait_send()
+        by_copy(n).wait_send()
     ay.wait_send()
     a_drain()
     b_drain()
@@ -463,7 +486,7 @@
         V((KC, 256, width // KC), BF),
         V((KC, width * 4 // KC, HS), BF),
         V((width, 512), BF),
-        V((256, 512), F32),
+        V((256, 256), F32),
         V((NZ, 2, 256, 256), BF),
         V((2, 2, 256, 256), BF),
         V((NZ, 8, 256), F32),
@@ -480,8 +503,8 @@
         V((256, 512), BF),
         V((256, 512), BF),
         V((256, 512), BF),
-        V((8, 256, 512), BF),
-        V((8, 256, 512), BF),
+        V((NX, 2, 256, 512), BF),
+        V((NX, 2, 256, 512), BF),
         V((NX, 2, 256, 512), BF),
         V((NX, rest, 512), BF),
         V((NX, rest, 512), BF),
@@ -493,15 +516,15 @@
         V((ROWS_A, 512), BF),
         V((256, 256), BF),
         D((2, KC)),
-        D((2, 2, 4)), D((2, 2, 4)),
+        D((2, 4, 4)), D((2, 4, 4)),
         D((2,)), D((2,)),
         D((NZ,)), D((NZ,)),
         D((NZ,)), D((NZ,)),
         D((NZ,)), D((NZ,)),
         D((NZ,)), D((NZ,)),
         D, D,
-        D((8,)), D((8,)),
-        D, D,
+        D((NX, 2)), D((NX, 2)),
+        D((NX,)), D((NX,)),
         D((6,)), D((6,)),
         D((6,)), D((6,)),
         D, D,

time: 90 us -> 78.5 us (0.87); the launches traced: 88.4 us -> 78.3 us
  Pallas kernels: 84.6 us -> 74.5 us
    pallas_call x1, Pallas kernels: 84.6 us -> 74.5 us  [on_device(): pl.pallas_call(kernel, out_shape=(jax.ShapeDtypeStruct((256, 256), BF), j...]
where the time goes in v3:
time: 78.5 us; the launch traced here: 78.3 us
  Pallas kernels  74.5 us (95%)
  local copies, waits for them, and re-layouts  3.24 us (4%)
    pallas_call x1, Pallas kernels, on_device(): pl.pallas_call(kernel, out_shape=(jax.ShapeDtypeStruct((256, 256), BF), j...  74.5 us
    unnamed x2, local copies, waits for them, and re-layouts  3.24 us

profile of v3, /device:TPU:1, one launch (start us, length us, event | category | flops | bytes accessed | tf_op | source)
XLA Modules:
  0.0 78.3 jit_solution(10937004575058042749)
XLA Ops:
  0.6 74.5 %shard_map.68 = (bf16[256,256]{1,0:T(8,128)(2,1)}, bf16[256,512]{1,0:T(8,128)(2,1)}) custom-call(s32[2,4]{1,0:T(2,128)} %bitcast.7, bf16[256,256]{1,0:T(8,128)(2,1)} %q_ref.1, bf16[256,256]{1,0:T(8,128)(2,1)} %g_ref.1, bf16[256,8192]{1,0:T(8,128)(2,1)} %x_hbm.1, bf16[32768,128]{1,0:T(8,128)(2,1)} %bitcast.6), custom_call_target="tpu_custom_call" | custom-call | flops 6000000000 | bytes 13631488 | tf_op jit(solution)/shard_map/pallas_call | solution.py:534
  75.1 1.6 %copy.10 = bf16[256,256]{1,0:T(8,128)(2,1)} copy(bf16[256,256]{1,0:T(8,128)(2,1)} %get-tuple-element.4) | data formatting | bytes 262144
  76.7 1.7 %copy.11 = bf16[256,512]{1,0:T(8,128)(2,1)} copy(bf16[256,512]{1,0:T(8,128)(2,1)} %get-tuple-element.5) | data formatting | bytes 524288

commit v4 on v3

--- a/solution.py
+++ b/solution.py
@@ -27,11 +27,11 @@
 
 
 def kernel(
-    cit_ref, q_ref, g_ref, x_hbm, w_hbm, att_ref, nbr_ref,
+    cit_ref, q_hbm, g_hbm, x_hbm, w_hbm, att_ref, nbr_ref,
     X, W32, W, acc, G, KV, info_out, info_in, E, DP, st_out, st_in, res_out, res_in,
     at_out, at_in, GR, yg_out, yg_in, kvg, cs_out, cs_in, R, by_in, RB,
     ax_in, ax_tmp, bx_in, bx_tmp, ay_out, ay_in, PM,
-    ld_sem, ag_send, ag_recv, kv_send, kv_recv, inf_send, inf_recv, st_send, st_recv,
+    ld_sem, own_sem, ag_send, ag_recv, kv_send, kv_recv, inf_send, inf_recv, st_send, st_recv,
     rs_send, rs_recv, at_send, at_recv, yg_send, yg_recv, cs_send, cs_recv,
     by_send, by_recv, ax_send, ax_recv, bx_send, bx_recv, ay_send, ay_recv,
 ):
@@ -66,6 +66,10 @@
             w_hbm.at[pl.ds(pl.multiple_of(k * 4 * depth, depth), 4 * depth), :], W32.at[k], ld_sem.at[0, k]
         )
 
+    own_rows = [pltpu.make_async_copy(src, G.at[z, i], own_sem.at[i]) for i, src in enumerate([q_hbm, g_hbm])]
+    for cp in own_rows:
+        cp.start()
+
     def start_loads(k, _):
         w_load(k).start()
         x_load(k).start()
@@ -79,8 +83,6 @@
     ]:
         pl.semaphore_signal(barrier, inc=1, device_id=dev, device_id_type=pl.DeviceIdType.MESH)
 
-    G[z, 0] = q_ref[...]
-    G[z, 1] = g_ref[...]
     lane = lax.broadcasted_iota(jnp.int32, (16, 256), 1) // CH
     owner = lax.broadcasted_iota(jnp.int32, (16, 256), 0)
     ids = []
@@ -101,6 +103,8 @@
             info_out[t, 2 + w : 3 + w, :] = sel[o : o + 1]
         info_out[t, 4:8, :] = jnp.zeros((4, 256), F32)
     info_in[z] = info_out[z]
+    for cp in own_rows:
+        cp.wait()
     pl.semaphore_wait(barrier, 12)
 
     def ag(direction, u, t):
@@ -189,6 +193,7 @@
     relay(2, 3)
     lax.fori_loop(1, NZ, info_wait, 0)
     relay(3, 0)
+    relay(3, 1)
     for h in range(2):
         kv_wait(h)
 
@@ -235,7 +240,6 @@
 
         lax.fori_loop(0, 1 if t == 4 else 2, side, 0)
 
-    relay(3, 1)
     att1(z)
     both(1)
     both(2)
@@ -326,33 +330,24 @@
     two, nxt, prv = lax.rem(x + 2, NX), lax.rem(x + 1, NX), lax.rem(x + 3, NX)
     order = [two, nxt, prv, x]
 
-    def product(n, core, yl):
-        e = (order[n] * 2 + core) * 2 + yl
+    def product(p, n, core):
+        e = (order[n] * 2 + core) * 2 + (1 - m if p == 0 else m)
         return dot(kvg[...], W[pl.ds(pl.multiple_of(e * 512, 512), 512), :], NT)
 
-    def cs_copy(n, yl):
-        return remote(cs_out.at[n, yl], cs_in.at[n, yl], cs_send.at[n, yl], cs_recv.at[n, yl], core_mate)
-
-    def for_mate(n):
-        def one(yl, _):
-            cs_out[n, yl] = product(n, 1 - c, yl).astype(BF)
-            cs_copy(n, yl).start()
-            return 0
-
-        lax.fori_loop(0, 2, one, 0)
+    def cs_copy(p, n):
+        return remote(cs_out.at[p, n], cs_in.at[p, n], cs_send.at[p, n], cs_recv.at[p, n], core_mate)
+
+    def for_mate(p, n):
+        cs_out[p, n] = product(p, n, 1 - c).astype(BF)
+        cs_copy(p, n).start()
+
+    def own(p, n):
+        mine = product(p, n, c)
+        cs_copy(p, n).wait_recv()
+        R[p, n] = (mine + cs_in[p, n].astype(F32)).astype(BF)
 
     def by_copy(n):
-        return remote(R.at[n, 1 - m, ROWS_A:256, :], by_in.at[n], by_send.at[n], by_recv.at[n], m_mate)
-
-    def own(n):
-        def one(yl, _):
-            mine = product(n, c, yl)
-            cs_copy(n, yl).wait_recv()
-            R[n, yl] = (mine + cs_in[n, yl].astype(F32)).astype(BF)
-            return 0
-
-        lax.fori_loop(0, 2, one, 0)
-        by_copy(n).start()
+        return remote(R.at[0, n, ROWS_A:256, :], by_in.at[n], by_send.at[n], by_recv.at[n], m_mate)
 
     def xsum(src, tmp, into, ssem, rsem):
         def at(n, half):
@@ -398,8 +393,13 @@
 
         return start, relay, finish, drain
 
-    a_start, a_relay, a_finish, a_drain = xsum(
-        lambda n, cols: R.at[n, :, 0:ROWS_A, cols], ax_tmp, ax_in, ax_send, ax_recv
+    a0_start, a0_relay, a0_finish, a0_drain = xsum(
+        lambda n, cols: R.at[0, n, 0:ROWS_A, cols],
+        ax_tmp.at[0], ax_in.at[0], ax_send.at[0], ax_recv.at[0],
+    )
+    a1_start, a1_relay, a1_finish, a1_drain = xsum(
+        lambda n, cols: R.at[1, n, 0:ROWS_A, cols],
+        ax_tmp.at[1], ax_in.at[1], ax_send.at[1], ax_recv.at[1],
     )
     b_start, b_relay, b_finish, b_drain = xsum(
         lambda n, cols: RB.at[n, :, cols], bx_tmp, bx_in, bx_send, bx_recv
@@ -407,29 +407,29 @@
 
     def add_b(n):
         by_copy(n).wait_recv()
-        RB[n] = (R[n, m, ROWS_A:256, :].astype(F32) + by_in[n].astype(F32)).astype(BF)
+        RB[n] = (R[1, n, ROWS_A:256, :].astype(F32) + by_in[n].astype(F32)).astype(BF)
         b_start(n)
 
-    for_mate(0)
-    for_mate(1)
-    own(0)
-    a_start(0)
-    for_mate(2)
-    own(1)
-    a_start(1)
-    for_mate(3)
-    own(2)
-    a_start(2)
-    a_relay()
-    own(3)
+    ay = remote(ay_out, ay_in, ay_send, ay_recv, m_mate)
+    for_mate(0, 0)
+    for_mate(0, 1)
     for n in range(NX):
+        own(0, n)
+        a0_start(n)
+        by_copy(n).start()
+        for_mate(*((0, n + 2) if n < 2 else (1, n - 2)))
+    a0_relay()
+    for n in range(NX):
+        own(1, n)
+        a1_start(n)
+        if n < 2:
+            for_mate(1, n + 2)
         add_b(n)
-    fa = a_finish()
+    fa = a0_finish()
     for half in range(2):
-        cols = slice(half * 256, half * 256 + 256)
-        ay_out[:, :, cols] = fa[half].astype(BF)
-    ay = remote(ay_out.at[1 - m], ay_in, ay_send, ay_recv, m_mate)
+        ay_out[:, half * 256 : half * 256 + 256] = fa[half].astype(BF)
     ay.start()
+    a1_relay()
     b_relay()
 
     def at_wait(r, _):
@@ -447,8 +447,11 @@
     for half in range(2):
         cols = slice(half * 256, half * 256 + 256)
         nbr_ref[ROWS_A:256, cols] = fb[half].astype(BF)
+    fa = a1_finish()
     ay.wait_recv()
-    nbr_ref[0:ROWS_A, :] = (ay_out[m].astype(F32) + ay_in[...].astype(F32)).astype(BF)
+    for half in range(2):
+        cols = slice(half * 256, half * 256 + 256)
+        nbr_ref[0:ROWS_A, cols] = (fa[half] + ay_in[:, cols].astype(F32)).astype(BF)
 
     for direction in range(2):
         for u in range(4):
@@ -469,12 +472,24 @@
     yg.wait_send()
 
     for n in range(NX):
-        for yl in range(2):
-            cs_copy(n, yl).wait_send()
+        for p in range(2):
+            cs_copy(p, n).wait_send()
         by_copy(n).wait_send()
     ay.wait_send()
-    a_drain()
+    a0_drain()
+    a1_drain()
     b_drain()
+
+
+def hand_over(att_from, nbr_from, att_to, nbr_to, sem):
+    copies = [
+        pltpu.make_async_copy(att_from, att_to, sem.at[0]),
+        pltpu.make_async_copy(nbr_from, nbr_to, sem.at[1]),
+    ]
+    for cp in copies:
+        cp.start()
+    for cp in copies:
+        cp.wait()
 
 
 def on_device(nbr_states, kv_weight, queries, out_grad, citations):
@@ -503,19 +518,20 @@
         V((256, 512), BF),
         V((256, 512), BF),
         V((256, 512), BF),
-        V((NX, 2, 256, 512), BF),
-        V((NX, 2, 256, 512), BF),
-        V((NX, 2, 256, 512), BF),
+        V((2, NX, 256, 512), BF),
+        V((2, NX, 256, 512), BF),
+        V((2, NX, 256, 512), BF),
         V((NX, rest, 512), BF),
         V((NX, rest, 512), BF),
-        V((6, 2, ROWS_A, 256), BF),
+        V((2, 6, ROWS_A, 256), BF),
         V((2, 2, ROWS_A, 256), BF),
         V((6, rest, 256), BF),
         V((2, rest, 256), BF),
-        V((2, ROWS_A, 512), BF),
+        V((ROWS_A, 512), BF),
         V((ROWS_A, 512), BF),
         V((256, 256), BF),
         D((2, KC)),
+        D((2,)),
         D((2, 4, 4)), D((2, 4, 4)),
         D((2,)), D((2,)),
         D((NZ,)), D((NZ,)),
@@ -523,21 +539,19 @@
         D((NZ,)), D((NZ,)),
         D((NZ,)), D((NZ,)),
         D, D,
-        D((NX, 2)), D((NX, 2)),
+        D((2, NX)), D((2, NX)),
         D((NX,)), D((NX,)),
-        D((6,)), D((6,)),
+        D((2, 6)), D((2, 6)),
         D((6,)), D((6,)),
         D, D,
     ]
     vmem = pl.BlockSpec(memory_space=pltpu.VMEM)
     hbm = pl.BlockSpec(memory_space=pl.ANY)
-    return pl.pallas_call(
+    shapes = (jax.ShapeDtypeStruct((256, 256), BF), jax.ShapeDtypeStruct((256, 512), BF))
+    results = pl.pallas_call(
         kernel,
-        out_shape=(
-            jax.ShapeDtypeStruct((256, 256), BF),
-            jax.ShapeDtypeStruct((256, 512), BF),
-        ),
-        in_specs=[pl.BlockSpec(memory_space=pltpu.SMEM), vmem, vmem, hbm, hbm],
+        out_shape=shapes,
+        in_specs=[pl.BlockSpec(memory_space=pltpu.SMEM), hbm, hbm, hbm, hbm],
         out_specs=(vmem, vmem),
         scratch_shapes=scratch,
         compiler_params=pltpu.CompilerParams(
@@ -547,6 +561,13 @@
             flops=6 * 10**9, bytes_accessed=13 * 2**20, transcendentals=2 * 10**6
         ),
     )(citations.T, queries, out_grad, nbr_states, weight)
+    return pl.pallas_call(
+        hand_over,
+        out_shape=shapes,
+        in_specs=[hbm, hbm],
+        out_specs=(hbm, hbm),
+        scratch_shapes=[D((2,))],
+    )(*results)
 
 
 def solution(mesh):

time: 78.5 us -> 87.2 us (1.11)
  Pallas kernels: 74.5 us -> 86.5 us
  local copies, waits for them, and re-layouts: 3.24 us -> 0 us
    pallas_call x1 -> x2, Pallas kernels: 74.5 us -> 86.5 us  [the longest x1 73.5 us: on_device(): pl.pallas_call(kernel, out_shape=shapes, in_specs=[pl.BlockSpec(memory_sp...]
    unnamed x2 -> x0, local copies, waits for them, and re-layouts: 3.24 us -> none
where the time goes in v4:
time: 87.2 us; the launch traced here: 87.1 us
  Pallas kernels  86.5 us (99%)
    pallas_call x1, Pallas kernels, on_device(): pl.pallas_call(kernel, out_shape=shapes, in_specs=[pl.BlockSpec(memory_sp...  73.5 us
    pallas_call x1, Pallas kernels, on_device(): pl.pallas_call(hand_over, out_shape=shapes, in_specs=[hbm, hbm], out_spec...  13 us

profile of v4, /device:TPU:1, one launch (start us, length us, event | category | flops | bytes accessed | tf_op | source)
XLA Modules:
  0.0 87.1 jit_solution(8595225002250347070)
XLA Ops:
  0.6 73.5 %shard_map.68 = (bf16[256,256]{1,0:T(8,128)(2,1)}, bf16[256,512]{1,0:T(8,128)(2,1)}) custom-call(s32[2,4]{1,0:T(2,128)} %bitcast.7, bf16[256,256]{1,0:T(8,128)(2,1)} %q_hbm.1, bf16[256,256]{1,0:T(8,128)(2,1)} %g_hbm.1, bf16[256,8192]{1,0:T(8,128)(2,1)} %x_hbm.1, bf16[32768,128]{1,0:T(8,128)(2,1)} %bitcast.6), custom_call_target="tpu_custom_call" | custom-call | flops 6000000000 | bytes 13631488 | tf_op jit(solution)/shard_map/pallas_call | solution.py:551
  74.1 13.0 %shard_map.69 = (bf16[256,256]{1,0:T(8,128)(2,1)}, bf16[256,512]{1,0:T(8,128)(2,1)}) custom-call(bf16[256,256]{1,0:T(8,128)(2,1)} %get-tuple-element.4.att_from, bf16[256,512]{1,0:T(8,128)(2,1)} %get-tuple-element.5.nbr_from), custom_call_target="tpu_custom_call" | custom-call | tf_op jit(solution)/shard_map/pallas_call | solution.py:564

commit v5 on v4

--- a/solution.py
+++ b/solution.py
@@ -30,7 +30,7 @@
     cit_ref, q_hbm, g_hbm, x_hbm, w_hbm, att_ref, nbr_ref,
     X, W32, W, acc, G, KV, info_out, info_in, E, DP, st_out, st_in, res_out, res_in,
     at_out, at_in, GR, yg_out, yg_in, kvg, cs_out, cs_in, R, by_in, RB,
-    ax_in, ax_tmp, bx_in, bx_tmp, ay_out, ay_in, PM,
+    ax_in, ax_tmp, bx_in, bx_tmp, ay_out, ay_in, PM, PRE,
     ld_sem, own_sem, ag_send, ag_recv, kv_send, kv_recv, inf_send, inf_recv, st_send, st_recv,
     rs_send, rs_recv, at_send, at_recv, yg_send, yg_recv, cs_send, cs_recv,
     by_send, by_recv, ax_send, ax_recv, bx_send, bx_recv, ay_send, ay_recv,
@@ -276,26 +276,29 @@
     def res_copy(r):
         return remote(res_out, res_in.at[z], rs_send.at[r], rs_recv.at[r], at_z(lax.rem(z + r, NZ)))
 
-    def res_start(r, _):
+    for r in (4, 5, 3, 6, 2, 7, 1):
         res_copy(r).start()
-        return 0
-
-    lax.fori_loop(1, NZ, res_start, 0)
     GR[...] = jnp.zeros_like(GR)
 
     def at_copy(j):
         r = lax.rem(j - z + NZ, NZ)
         return remote(at_out.at[j], at_in.at[z], at_send.at[r], at_recv.at[r], at_z(j))
 
-    def att2(r, _):
-        j = lax.rem(z + NZ - r, NZ)
-
-        @pl.when(r > 0)
-        def _():
-            remote(res_out, res_in.at[j], rs_send.at[r], rs_recv.at[r], at_z(j)).wait_recv()
-
-        for h in range(2):
-            cols = slice(h * HS, h * HS + HS)
+    def yg_copy(h):
+        return remote(yg_out.at[h], yg_in.at[h], yg_send.at[h], yg_recv.at[h], y_mate)
+
+    for h in range(2):
+        cols = slice(h * HS, h * HS + HS)
+        wide = slice(h * 256, h * 256 + 256)
+
+        def att2(r, _):
+            j = lax.rem(z + NZ - r, NZ)
+            if h == 0:
+
+                @pl.when(r > 0)
+                def _():
+                    remote(res_out, res_in.at[j], rs_send.at[r], rs_recv.at[r], at_z(j)).wait_recv()
+
             f = jnp.exp(st_out[j, 3 * h : 3 * h + 1, :] - res_in[j, 3 * h : 3 * h + 1, :])
             p = E[j, h] * (f * res_in[j, 3 * h + 1 : 3 * h + 2, :])
             rounded = p.astype(BF)
@@ -306,43 +309,61 @@
             for w in range(2):
                 one = info_in[j, 2 + w : 3 + w, :]
                 mine = part[w * CL : w * CL + CL]
-                GR[w, 0:CL, h * 256 : h * 256 + 256] += mine * (1.0 - one)
-                GR[w, CL : 2 * CL, h * 256 : h * 256 + 256] += mine * one
+                GR[w, 0:CL, wide] += mine * (1.0 - one)
+                GR[w, CL : 2 * CL, wide] += mine * one
             values = chosen(j, h)[:, HS:]
             at_out[j, cols, :] = dot(values, rounded, TN).astype(BF)
-        return 0
-
-    lax.fori_loop(0, NZ, att2, 0)
-    at_in[z] = at_out[z]
-
-    yg_out[...] = GR[1 - yh].astype(BF)
-    yg = remote(yg_out, yg_in, yg_send, yg_recv, y_mate)
-    yg.start()
+            return 0
+
+        lax.fori_loop(0, NZ, att2, 0)
+        yg_out[h] = GR[1 - yh, :, wide].astype(BF)
+        yg_copy(h).start()
 
     def at_start(r, _):
         at_copy(lax.rem(z + r, NZ)).start()
         return 0
 
     lax.fori_loop(1, NZ, at_start, 0)
-    yg.wait_recv()
-    kvg[...] = (GR[yh] + yg_in[...].astype(F32)).astype(BF)
+    at_in[z] = at_out[z]
+
+    def add_mate(h):
+        wide = slice(h * 256, h * 256 + 256)
+        yg_copy(h).wait_recv()
+        kvg[:, wide] = (GR[yh, :, wide] + yg_in[h].astype(F32)).astype(BF)
+
+    add_mate(0)
 
     two, nxt, prv = lax.rem(x + 2, NX), lax.rem(x + 1, NX), lax.rem(x + 3, NX)
     order = [two, nxt, prv, x]
 
-    def product(p, n, core):
+    def w_rows(p, n, core):
         e = (order[n] * 2 + core) * 2 + (1 - m if p == 0 else m)
-        return dot(kvg[...], W[pl.ds(pl.multiple_of(e * 512, 512), 512), :], NT)
+        return pl.ds(pl.multiple_of(e * 512, 512), 512)
+
+    def half(p, n, core, h):
+        wide = slice(h * 256, h * 256 + 256)
+        return dot(kvg[:, wide], W[w_rows(p, n, core), wide], NT)
+
+    early = {(0, 0, 0): 0, (0, 1, 0): 1, (0, 0, 1): 2}
+    for (p, n, mine), i in early.items():
+        PRE[i] = half(p, n, c if mine else 1 - c, 0)
+    add_mate(1)
+
+    def product(p, n, mine):
+        core = c if mine else 1 - c
+        if (p, n, mine) in early:
+            return PRE[early[p, n, mine]] + half(p, n, core, 1)
+        return dot(kvg[...], W[w_rows(p, n, core), :], NT)
 
     def cs_copy(p, n):
         return remote(cs_out.at[p, n], cs_in.at[p, n], cs_send.at[p, n], cs_recv.at[p, n], core_mate)
 
     def for_mate(p, n):
-        cs_out[p, n] = product(p, n, 1 - c).astype(BF)
+        cs_out[p, n] = product(p, n, 0).astype(BF)
         cs_copy(p, n).start()
 
     def own(p, n):
-        mine = product(p, n, c)
+        mine = product(p, n, 1)
         cs_copy(p, n).wait_recv()
         R[p, n] = (mine + cs_in[p, n].astype(F32)).astype(BF)
 
@@ -424,13 +445,16 @@
         a1_start(n)
         if n < 2:
             for_mate(1, n + 2)
-        add_b(n)
+    add_b(0)
     fa = a0_finish()
-    for half in range(2):
-        ay_out[:, half * 256 : half * 256 + 256] = fa[half].astype(BF)
+    for half_ in range(2):
+        ay_out[:, half_ * 256 : half_ * 256 + 256] = fa[half_].astype(BF)
     ay.start()
     a1_relay()
+    add_b(1)
+    add_b(2)
     b_relay()
+    add_b(3)
 
     def at_wait(r, _):
         src = lax.rem(z + NZ - r, NZ)
@@ -469,7 +493,8 @@
         return 0
 
     lax.fori_loop(1, NZ, sent, 0)
-    yg.wait_send()
+    for h in range(2):
+        yg_copy(h).wait_send()
 
     for n in range(NX):
         for p in range(2):
@@ -481,15 +506,9 @@
     b_drain()
 
 
-def hand_over(att_from, nbr_from, att_to, nbr_to, sem):
-    copies = [
-        pltpu.make_async_copy(att_from, att_to, sem.at[0]),
-        pltpu.make_async_copy(nbr_from, nbr_to, sem.at[1]),
-    ]
-    for cp in copies:
-        cp.start()
-    for cp in copies:
-        cp.wait()
+def hand_over(att_from, nbr_from, att_to, nbr_to):
+    att_to[...] = att_from[...]
+    nbr_to[...] = nbr_from[...]
 
 
 def on_device(nbr_states, kv_weight, queries, out_grad, citations):
@@ -515,8 +534,8 @@
         V((NZ, 256, 256), BF),
         V((NZ, 256, 256), BF),
         V((2, 256, 512), F32),
-        V((256, 512), BF),
-        V((256, 512), BF),
+        V((2, 256, 256), BF),
+        V((2, 256, 256), BF),
         V((256, 512), BF),
         V((2, NX, 256, 512), BF),
         V((2, NX, 256, 512), BF),
@@ -530,6 +549,7 @@
         V((ROWS_A, 512), BF),
         V((ROWS_A, 512), BF),
         V((256, 256), BF),
+        V((3, 256, 512), F32),
         D((2, KC)),
         D((2,)),
         D((2, 4, 4)), D((2, 4, 4)),
@@ -538,7 +558,7 @@
         D((NZ,)), D((NZ,)),
         D((NZ,)), D((NZ,)),
         D((NZ,)), D((NZ,)),
-        D, D,
+        D((2,)), D((2,)),
         D((2, NX)), D((2, NX)),
         D((NX,)), D((NX,)),
         D((2, 6)), D((2, 6)),
@@ -564,9 +584,8 @@
     return pl.pallas_call(
         hand_over,
         out_shape=shapes,
-        in_specs=[hbm, hbm],
-        out_specs=(hbm, hbm),
-        scratch_shapes=[D((2,))],
+        in_specs=[vmem, vmem],
+        out_specs=(vmem, vmem),
     )(*results)
 
 

time: 87.2 us -> 75.5 us (0.87)
  Pallas kernels: 86.5 us -> 74.7 us
    pallas_call x1, Pallas kernels: 13 us -> 1.78 us  [on_device(): pl.pallas_call(hand_over, out_shape=shapes, in_specs=[vmem, vmem], out_sp...]
where the time goes in v5:
time: 75.5 us; the launch traced here: 75.4 us
  Pallas kernels  74.7 us (99%)
    pallas_call x1, Pallas kernels, on_device(): pl.pallas_call(kernel, out_shape=shapes, in_specs=[pl.BlockSpec(memory_sp...  73 us
    pallas_call x1, Pallas kernels, on_device(): pl.pallas_call(hand_over, out_shape=shapes, in_specs=[vmem, vmem], out_sp...  1.78 us

profile of v5, /device:TPU:1, one launch (start us, length us, event | category | flops | bytes accessed | tf_op | source)
XLA Modules:
  0.0 75.4 jit_solution(8544598391980427956)
XLA Ops:
  0.6 73.0 %shard_map.68 = (bf16[256,256]{1,0:T(8,128)(2,1)}, bf16[256,512]{1,0:T(8,128)(2,1)}) custom-call(s32[2,4]{1,0:T(2,128)} %bitcast.7, bf16[256,256]{1,0:T(8,128)(2,1)} %q_hbm.1, bf16[256,256]{1,0:T(8,128)(2,1)} %g_hbm.1, bf16[256,8192]{1,0:T(8,128)(2,1)} %x_hbm.1, bf16[32768,128]{1,0:T(8,128)(2,1)} %bitcast.6), custom_call_target="tpu_custom_call" | custom-call | flops 6000000000 | bytes 13631488 | tf_op jit(solution)/shard_map/pallas_call | solution.py:571
  73.6 1.8 %shard_map.69 = (bf16[256,256]{1,0:T(8,128)(2,1)}, bf16[256,512]{1,0:T(8,128)(2,1)}) custom-call(bf16[256,256]{1,0:T(8,128)(2,1)} %get-tuple-element.4.att_from, bf16[256,512]{1,0:T(8,128)(2,1)} %get-tuple-element.5.nbr_from), custom_call_target="tpu_custom_call" | custom-call | tf_op jit(solution)/shard_map/pallas_call | solution.py:584

commit v6 on v5

--- a/solution.py
+++ b/solution.py
@@ -29,10 +29,10 @@
 def kernel(
     cit_ref, q_hbm, g_hbm, x_hbm, w_hbm, att_ref, nbr_ref,
     X, W32, W, acc, G, KV, info_out, info_in, E, DP, st_out, st_in, res_out, res_in,
-    at_out, at_in, GR, yg_out, yg_in, kvg, cs_out, cs_in, R, by_in, RB,
+    far_in, at_out, at_in, GR, yg_out, yg_in, kvg, cs_out, cs_in, R, by_in, RB,
     ax_in, ax_tmp, bx_in, bx_tmp, ay_out, ay_in, PM, PRE,
     ld_sem, own_sem, ag_send, ag_recv, kv_send, kv_recv, inf_send, inf_recv, st_send, st_recv,
-    rs_send, rs_recv, at_send, at_recv, yg_send, yg_recv, cs_send, cs_recv,
+    rs_send, rs_recv, far_send, far_recv, at_send, at_recv, yg_send, yg_recv, cs_send, cs_recv,
     by_send, by_recv, ax_send, ax_recv, bx_send, bx_recv, ay_send, ay_recv,
 ):
     s, d, m = lax.axis_index("section"), lax.axis_index("dp"), lax.axis_index("mp")
@@ -238,38 +238,43 @@
             st_copy(j).start()
             return 0
 
-        lax.fori_loop(0, 1 if t == 4 else 2, side, 0)
-
-    att1(z)
+        lax.fori_loop(0, 2, side, 0)
+
+    far = lax.rem(z + 4, NZ)
+
+    def far_copy(r):
+        return remote(st_out.at[far], far_in.at[far], far_send.at[r], far_recv.at[r], at_z(lax.rem(z + r, NZ)))
+
     both(1)
     both(2)
     arrived(2, 2)
     arrived(2, 3)
     both(3)
+    att1(z)
     arrived(3, 0)
     arrived(3, 1)
-    both(4)
-
+    att1(far)
+    far_in[far] = st_out[far]
+    for r in (4, 5, 3, 6, 2, 7, 1):
+        far_copy(r).start()
+
+    near = (0, 1, 2, 3, 5, 6, 7)
     st_in[z] = st_out[z]
-
-    def st_wait(r, _):
+    for r in near[1:]:
         src = lax.rem(z + NZ - r, NZ)
         remote(st_out.at[src], st_in.at[src], st_send.at[r], st_recv.at[r], at_z(src)).wait_recv()
-        return 0
-
-    lax.fori_loop(1, NZ, st_wait, 0)
     for h in range(2):
-        tops = [st_in[i, 3 * h : 3 * h + 1, :] for i in range(NZ)]
-        top = functools.reduce(jnp.maximum, tops)
+        stats = [[st_in[lax.rem(z + NZ - r, NZ), 3 * h + i : 3 * h + i + 1, :] for i in range(3)] for r in near]
+        top = functools.reduce(jnp.maximum, [v[0] for v in stats])
         total = jnp.zeros((1, 256), F32)
         dots = jnp.zeros((1, 256), F32)
-        for i in range(NZ):
-            f = jnp.exp(tops[i] - top)
-            total += f * st_in[i, 3 * h + 1 : 3 * h + 2, :]
-            dots += f * st_in[i, 3 * h + 2 : 3 * h + 3, :]
+        for v in stats:
+            f = jnp.exp(v[0] - top)
+            total += f * v[1]
+            dots += f * v[2]
         res_out[3 * h : 3 * h + 1, :] = top
-        res_out[3 * h + 1 : 3 * h + 2, :] = 1.0 / total
-        res_out[3 * h + 2 : 3 * h + 3, :] = dots / total
+        res_out[3 * h + 1 : 3 * h + 2, :] = total
+        res_out[3 * h + 2 : 3 * h + 3, :] = dots
     res_out[6:8, :] = jnp.zeros((2, 256), F32)
     res_in[z] = res_out[...]
 
@@ -299,10 +304,22 @@
                 def _():
                     remote(res_out, res_in.at[j], rs_send.at[r], rs_recv.at[r], at_z(j)).wait_recv()
 
-            f = jnp.exp(st_out[j, 3 * h : 3 * h + 1, :] - res_in[j, 3 * h : 3 * h + 1, :])
-            p = E[j, h] * (f * res_in[j, 3 * h + 1 : 3 * h + 2, :])
+                @pl.when(r != 4)
+                def _():
+                    k = lax.rem(r + 4, NZ)
+                    remote(st_out.at[j], far_in.at[j], far_send.at[k], far_recv.at[k], at_z(j)).wait_recv()
+
+            tops = [ref[j, 3 * h : 3 * h + 1, :] for ref in (res_in, far_in)]
+            top = jnp.maximum(tops[0], tops[1])
+            fs = [jnp.exp(v - top) for v in tops]
+            total, dots = [
+                fs[0] * res_in[j, 3 * h + i : 3 * h + i + 1, :] + fs[1] * far_in[j, 3 * h + i : 3 * h + i + 1, :]
+                for i in (1, 2)
+            ]
+            share = 1.0 / total
+            p = E[j, h] * (jnp.exp(st_out[j, 3 * h : 3 * h + 1, :] - top) * share)
             rounded = p.astype(BF)
-            ds = (p * (DP[j, h] - res_in[j, 3 * h + 2 : 3 * h + 3, :])).astype(BF)
+            ds = (p * (DP[j, h] - dots * share)).astype(BF)
             kg = dot(ds, G[j, 0, :, cols], NN) * scaling
             vg = dot(rounded, G[j, 1, :, cols], NN)
             part = jnp.concatenate([kg, vg], axis=1)
@@ -344,7 +361,7 @@
         wide = slice(h * 256, h * 256 + 256)
         return dot(kvg[:, wide], W[w_rows(p, n, core), wide], NT)
 
-    early = {(0, 0, 0): 0, (0, 1, 0): 1, (0, 0, 1): 2}
+    early = {(0, 0, 0): 0, (0, 1, 0): 1, (0, 2, 0): 2, (0, 0, 1): 3}
     for (p, n, mine), i in early.items():
         PRE[i] = half(p, n, c if mine else 1 - c, 0)
     add_mate(1)
@@ -434,17 +451,18 @@
     ay = remote(ay_out, ay_in, ay_send, ay_recv, m_mate)
     for_mate(0, 0)
     for_mate(0, 1)
+    for_mate(0, 2)
     for n in range(NX):
         own(0, n)
         a0_start(n)
         by_copy(n).start()
-        for_mate(*((0, n + 2) if n < 2 else (1, n - 2)))
+        for_mate(*((0, 3) if n == 0 else (1, n - 1)))
     a0_relay()
     for n in range(NX):
         own(1, n)
         a1_start(n)
-        if n < 2:
-            for_mate(1, n + 2)
+        if n == 0:
+            for_mate(1, 3)
     add_b(0)
     fa = a0_finish()
     for half_ in range(2):
@@ -487,12 +505,14 @@
     def sent(r, _):
         j = lax.rem(z + r, NZ)
         info_copy(r).wait_send()
-        st_copy(j).wait_send()
         res_copy(r).wait_send()
+        far_copy(r).wait_send()
         at_copy(j).wait_send()
         return 0
 
     lax.fori_loop(1, NZ, sent, 0)
+    for r in near[1:]:
+        st_copy(lax.rem(z + r, NZ)).wait_send()
     for h in range(2):
         yg_copy(h).wait_send()
 
@@ -504,11 +524,6 @@
     a0_drain()
     a1_drain()
     b_drain()
-
-
-def hand_over(att_from, nbr_from, att_to, nbr_to):
-    att_to[...] = att_from[...]
-    nbr_to[...] = nbr_from[...]
 
 
 def on_device(nbr_states, kv_weight, queries, out_grad, citations):
@@ -531,6 +546,7 @@
         V((NZ, 8, 256), F32),
         V((8, 256), F32),
         V((NZ, 8, 256), F32),
+        V((NZ, 8, 256), F32),
         V((NZ, 256, 256), BF),
         V((NZ, 256, 256), BF),
         V((2, 256, 512), F32),
@@ -549,11 +565,12 @@
         V((ROWS_A, 512), BF),
         V((ROWS_A, 512), BF),
         V((256, 256), BF),
-        V((3, 256, 512), F32),
+        V((4, 256, 512), F32),
         D((2, KC)),
         D((2,)),
         D((2, 4, 4)), D((2, 4, 4)),
         D((2,)), D((2,)),
+        D((NZ,)), D((NZ,)),
         D((NZ,)), D((NZ,)),
         D((NZ,)), D((NZ,)),
         D((NZ,)), D((NZ,)),
@@ -567,10 +584,9 @@
     ]
     vmem = pl.BlockSpec(memory_space=pltpu.VMEM)
     hbm = pl.BlockSpec(memory_space=pl.ANY)
-    shapes = (jax.ShapeDtypeStruct((256, 256), BF), jax.ShapeDtypeStruct((256, 512), BF))
-    results = pl.pallas_call(
+    return pl.pallas_call(
         kernel,
-        out_shape=shapes,
+        out_shape=(pltpu.VMEM((256, 256), BF), pltpu.VMEM((256, 512), BF)),
         in_specs=[pl.BlockSpec(memory_space=pltpu.SMEM), hbm, hbm, hbm, hbm],
         out_specs=(vmem, vmem),
         scratch_shapes=scratch,
@@ -581,12 +597,6 @@
             flops=6 * 10**9, bytes_accessed=13 * 2**20, transcendentals=2 * 10**6
         ),
     )(citations.T, queries, out_grad, nbr_states, weight)
-    return pl.pallas_call(
-        hand_over,
-        out_shape=shapes,
-        in_specs=[vmem, vmem],
-        out_specs=(vmem, vmem),
-    )(*results)
 
 
 def solution(mesh):

time: 75.5 us -> 72.7 us (0.963)
  Pallas kernels: 74.7 us -> 70.6 us
  local copies, waits for them, and re-layouts: 0 us -> 1.36 us
    pallas_call x2 -> x1, Pallas kernels: 74.7 us -> 70.6 us  [on_device(): pl.pallas_call(kernel, out_shape=(pltpu.VMEM((256, 256), BF), pltpu.VMEM(...]
    unnamed x0 -> x2, local copies, waits for them, and re-layouts: none -> 1.36 us
where the time goes in v6:
time: 72.7 us; the launch traced here: 72.6 us
  Pallas kernels  70.6 us (97%)
  local copies, waits for them, and re-layouts  1.36 us (2%)
    pallas_call x1, Pallas kernels, on_device(): pl.pallas_call(kernel, out_shape=(pltpu.VMEM((256, 256), BF), pltpu.VMEM(...  70.6 us

profile of v6, /device:TPU:1, one launch (start us, length us, event | category | flops | bytes accessed | tf_op | source)
XLA Modules:
  0.0 72.6 jit_solution(18164192765433399934)
XLA Ops:
  0.6 70.6 %shard_map.68 = (bf16[256,256]{1,0:T(8,128)(2,1)S(1)}, bf16[256,512]{1,0:T(8,128)(2,1)S(1)}) custom-call(s32[2,4]{1,0:T(2,128)} %bitcast.7, bf16[256,256]{1,0:T(8,128)(2,1)} %q_hbm.1, bf16[256,256]{1,0:T(8,128)(2,1)} %g_hbm.1, bf16[256,8192]{1,0:T(8,128)(2,1)} %x_hbm.1, bf16[32768,128]{1,0:T(8,128)(2,1)} %bitcast.6), custom_call_target="tpu_custom_call" | custom-call | flops 6000000000 | bytes 13631488 | tf_op jit(solution)/shard_map/pallas_call | solution.py:587
  71.2 0.7 copy.10
  71.9 0.7 copy.11

commit v7 on v6

--- a/solution.py
+++ b/solution.py
@@ -56,32 +56,48 @@
             device_id=dev, device_id_type=pl.DeviceIdType.MESH,
         )
 
-    def x_load(k):
-        return pltpu.make_async_copy(
-            x_hbm.at[:, pl.ds(pl.multiple_of(k * depth, depth), depth)], X.at[k], ld_sem.at[1, k]
-        )
-
-    def w_load(k):
-        return pltpu.make_async_copy(
-            w_hbm.at[pl.ds(pl.multiple_of(k * 4 * depth, depth), 4 * depth), :], W32.at[k], ld_sem.at[0, k]
-        )
-
-    own_rows = [pltpu.make_async_copy(src, G.at[z, i], own_sem.at[i]) for i, src in enumerate([q_hbm, g_hbm])]
-    for cp in own_rows:
-        cp.start()
-
-    def start_loads(k, _):
-        w_load(k).start()
-        x_load(k).start()
-        return 0
-
-    lax.fori_loop(0, KC, start_loads, 0)
-
     barrier = pltpu.get_barrier_semaphore()
     for dev in [at_z(lax.rem(z + r, NZ)) for r in range(1, NZ)] + [
         y_mate, core_mate, x_right, x_left, m_mate
     ]:
         pl.semaphore_signal(barrier, inc=1, device_id=dev, device_id_type=pl.DeviceIdType.MESH)
+
+    def x_load(k):
+        return pltpu.make_async_copy(
+            x_hbm.at[:, pl.ds(pl.multiple_of(k * depth, depth), depth)], X.at[k], ld_sem.at[1, k]
+        )
+
+    def w_load(k):
+        return pltpu.make_async_copy(
+            w_hbm.at[pl.ds(pl.multiple_of(k * 4 * depth, depth), 4 * depth), :], W32.at[k], ld_sem.at[0, k]
+        )
+
+    own_rows = [pltpu.make_async_copy(src, G.at[z, i], own_sem.at[i]) for i, src in enumerate([q_hbm, g_hbm])]
+    for cp in own_rows:
+        cp.start()
+
+    def start_loads(k, _):
+        w_load(k).start()
+        x_load(k).start()
+        return 0
+
+    lax.fori_loop(0, KC, start_loads, 0)
+
+    for cp in own_rows:
+        cp.wait()
+    pl.semaphore_wait(barrier, 12)
+
+    def ag(direction, u, t):
+        if direction == 0:
+            home, to, arr = lax.rem(z - t + NZ, NZ), lax.rem(z + 1, NZ), u // 2
+        else:
+            home, to, arr = lax.rem(z + t, NZ), lax.rem(z + NZ - 1, NZ), 1 - u // 2
+        piece = G.at[home, arr, pl.ds(pl.multiple_of((u % 2) * 128, 128), 128)]
+        return remote(piece, piece, ag_send.at[direction, u, t], ag_recv.at[direction, u, t], at_z(to))
+
+    for u in range(4):
+        for direction in range(2):
+            ag(direction, u, 0).start()
 
     lane = lax.broadcasted_iota(jnp.int32, (16, 256), 1) // CH
     owner = lax.broadcasted_iota(jnp.int32, (16, 256), 0)
@@ -103,22 +119,6 @@
             info_out[t, 2 + w : 3 + w, :] = sel[o : o + 1]
         info_out[t, 4:8, :] = jnp.zeros((4, 256), F32)
     info_in[z] = info_out[z]
-    for cp in own_rows:
-        cp.wait()
-    pl.semaphore_wait(barrier, 12)
-
-    def ag(direction, u, t):
-        if direction == 0:
-            home, to, arr = lax.rem(z - t + NZ, NZ), lax.rem(z + 1, NZ), u // 2
-        else:
-            home, to, arr = lax.rem(z + t, NZ), lax.rem(z + NZ - 1, NZ), 1 - u // 2
-        piece = G.at[home, arr, pl.ds(pl.multiple_of((u % 2) * 128, 128), 128)]
-        return remote(piece, piece, ag_send.at[direction, u, t], ag_recv.at[direction, u, t], at_z(to))
-
-    for u in range(4):
-        for direction in range(2):
-            ag(direction, u, 0).start()
-
     def info_copy(r):
         to = lax.rem(z + r, NZ)
         return remote(info_out.at[to], info_in.at[z], inf_send.at[r], inf_recv.at[r], at_z(to))
@@ -194,8 +194,7 @@
     lax.fori_loop(1, NZ, info_wait, 0)
     relay(3, 0)
     relay(3, 1)
-    for h in range(2):
-        kv_wait(h)
+    kv_wait(0)
 
     def chosen(j, h):
         out = []
@@ -209,8 +208,8 @@
         r = lax.rem(j - z + NZ, NZ)
         return remote(st_out.at[j], st_in.at[z], st_send.at[r], st_recv.at[r], at_z(j))
 
-    def att1(j):
-        for h in range(2):
+    def att1(j, heads=(0, 1)):
+        for h in heads:
             kv = chosen(j, h)
             cols = slice(h * HS, h * HS + HS)
             sc = dot(kv[:, :HS], G[j, 0, :, cols], NT) * scaling
@@ -229,13 +228,15 @@
             st_out[j, 3 * h : 3 * h + 1, :] = top
             st_out[j, 3 * h + 1 : 3 * h + 2, :] = jnp.sum(e, axis=0, keepdims=True)
             st_out[j, 3 * h + 2 : 3 * h + 3, :] = jnp.sum(e * dp, axis=0, keepdims=True)
-        st_out[j, 6:8, :] = jnp.zeros((2, 256), F32)
-
-    def both(t):
+        if 1 in heads:
+            st_out[j, 6:8, :] = jnp.zeros((2, 256), F32)
+
+    def both(t, heads=(0, 1)):
         def side(i, _):
             j = lax.rem(z + NZ - t + 2 * i * t, NZ)
-            att1(j)
-            st_copy(j).start()
+            att1(j, heads)
+            if 1 in heads:
+                st_copy(j).start()
             return 0
 
         lax.fori_loop(0, 2, side, 0)
@@ -245,12 +246,16 @@
     def far_copy(r):
         return remote(st_out.at[far], far_in.at[far], far_send.at[r], far_recv.at[r], at_z(lax.rem(z + r, NZ)))
 
-    both(1)
-    both(2)
+    att1(z, (0,))
+    both(1, (0,))
+    both(2, (0,))
+    kv_wait(1)
+    both(2, (1,))
     arrived(2, 2)
     arrived(2, 3)
     both(3)
-    att1(z)
+    both(1, (1,))
+    att1(z, (1,))
     arrived(3, 0)
     arrived(3, 1)
     att1(far)
@@ -348,6 +353,22 @@
         yg_copy(h).wait_recv()
         kvg[:, wide] = (GR[yh, :, wide] + yg_in[h].astype(F32)).astype(BF)
 
+    for direction in range(2):
+        for u in range(4):
+            for t in range(4 if u < 2 else 3):
+                ag(direction, u, t).wait_send()
+    for h in range(2):
+        kv_copy(h).wait_send()
+
+    def sent(r, _):
+        info_copy(r).wait_send()
+        res_copy(r).wait_send()
+        far_copy(r).wait_send()
+        return 0
+
+    lax.fori_loop(1, NZ, sent, 0)
+    for r in near[1:]:
+        st_copy(lax.rem(z + r, NZ)).wait_send()
     add_mate(0)
 
     two, nxt, prv = lax.rem(x + 2, NX), lax.rem(x + 1, NX), lax.rem(x + 3, NX)
@@ -485,6 +506,18 @@
         total += at_in[i].astype(F32)
     att_ref[...] = total.T.astype(BF)
 
+    def at_sent(r, _):
+        at_copy(lax.rem(z + r, NZ)).wait_send()
+        return 0
+
+    lax.fori_loop(1, NZ, at_sent, 0)
+    for h in range(2):
+        yg_copy(h).wait_send()
+
+    for n in range(NX):
+        for p in range(2):
+            cs_copy(p, n).wait_send()
+        by_copy(n).wait_send()
     fb = b_finish()
     for half in range(2):
         cols = slice(half * 256, half * 256 + 256)
@@ -495,31 +528,6 @@
         cols = slice(half * 256, half * 256 + 256)
         nbr_ref[0:ROWS_A, cols] = (fa[half] + ay_in[:, cols].astype(F32)).astype(BF)
 
-    for direction in range(2):
-        for u in range(4):
-            for t in range(4 if u < 2 else 3):
-                ag(direction, u, t).wait_send()
-    for h in range(2):
-        kv_copy(h).wait_send()
-
-    def sent(r, _):
-        j = lax.rem(z + r, NZ)
-        info_copy(r).wait_send()
-        res_copy(r).wait_send()
-        far_copy(r).wait_send()
-        at_copy(j).wait_send()
-        return 0
-
-    lax.fori_loop(1, NZ, sent, 0)
-    for r in near[1:]:
-        st_copy(lax.rem(z + r, NZ)).wait_send()
-    for h in range(2):
-        yg_copy(h).wait_send()
-
-    for n in range(NX):
-        for p in range(2):
-            cs_copy(p, n).wait_send()
-        by_copy(n).wait_send()
     ay.wait_send()
     a0_drain()
     a1_drain()

time: 72.7 us -> 72 us (level)
  no operation moved by 1% of the time
where the time goes in v7:
time: 72 us; the launch traced here: 71.9 us
  Pallas kernels  69.9 us (97%)
  local copies, waits for them, and re-layouts  1.36 us (2%)
    pallas_call x1, Pallas kernels, on_device(): pl.pallas_call(kernel, out_shape=(pltpu.VMEM((256, 256), BF), pltpu.VMEM(...  69.9 us

profile of v7, /device:TPU:1, one launch (start us, length us, event | category | flops | bytes accessed | tf_op | source)
XLA Modules:
  0.0 71.9 jit_solution(5387947736657452684)
XLA Ops:
  0.6 69.9 %shard_map.68 = (bf16[256,256]{1,0:T(8,128)(2,1)S(1)}, bf16[256,512]{1,0:T(8,128)(2,1)S(1)}) custom-call(s32[2,4]{1,0:T(2,128)} %bitcast.7, bf16[256,256]{1,0:T(8,128)(2,1)} %q_hbm.1, bf16[256,256]{1,0:T(8,128)(2,1)} %g_hbm.1, bf16[256,8192]{1,0:T(8,128)(2,1)} %x_hbm.1, bf16[32768,128]{1,0:T(8,128)(2,1)} %bitcast.6), custom_call_target="tpu_custom_call" | custom-call | flops 6000000000 | bytes 13631488 | tf_op jit(solution)/shard_map/pallas_call | solution.py:595
  70.5 0.7 copy.10
  71.2 0.7 copy.11

commit v8 on v7

--- a/solution.py
+++ b/solution.py
@@ -301,7 +301,9 @@
         cols = slice(h * HS, h * HS + HS)
         wide = slice(h * 256, h * 256 + 256)
 
-        def att2(r, _):
+        def att2(i, _):
+            pair = i // 2
+            r = 2 + pair - 3 * (pair // 2) - 2 * (pair // 3) + 4 * (i % 2)
             j = lax.rem(z + NZ - r, NZ)
             if h == 0:
 

time: 72 us -> 72.7 us (level)
  no operation moved by 1% of the time
where the time goes in v8:
time: 72.7 us; the launch traced here: 72.6 us
  Pallas kernels  70.6 us (97%)
  local copies, waits for them, and re-layouts  1.36 us (2%)
    pallas_call x1, Pallas kernels, on_device(): pl.pallas_call(kernel, out_shape=(pltpu.VMEM((256, 256), BF), pltpu.VMEM(...  70.6 us

profile of v8, /device:TPU:1, one launch (start us, length us, event | category | flops | bytes accessed | tf_op | source)
XLA Modules:
  0.0 72.6 jit_solution(5631855704248284611)
XLA Ops:
  0.6 70.6 %shard_map.68 = (bf16[256,256]{1,0:T(8,128)(2,1)S(1)}, bf16[256,512]{1,0:T(8,128)(2,1)S(1)}) custom-call(s32[2,4]{1,0:T(2,128)} %bitcast.7, bf16[256,256]{1,0:T(8,128)(2,1)} %q_hbm.1, bf16[256,256]{1,0:T(8,128)(2,1)} %g_hbm.1, bf16[256,8192]{1,0:T(8,128)(2,1)} %x_hbm.1, bf16[32768,128]{1,0:T(8,128)(2,1)} %bitcast.6), custom_call_target="tpu_custom_call" | custom-call | flops 6000000000 | bytes 13631488 | tf_op jit(solution)/shard_map/pallas_call | solution.py:597
  71.2 0.7 copy.10
  71.9 0.7 copy.11
